TPU v7x, 512 devices: a whole 4x4x16 slice. The times are simulated.
512 devices in a mesh: mode: 64 (over z_lo, y, core), row: 8 (over z_hi, x).
Axes of the slice: x: 4, y: 4, z: 16 (z_hi: 2, z_lo: 8; z = z_hi * 8 + z_lo), core: 2. Of those that a mesh axis runs over, the one named last changes fastest.
Arguments:
- forward: bfloat16 [64, 2, 1024, 1024], P('mode', None, 'row'), may hold values from -8 to 8
- backward_first: bfloat16 [64, 2, 1024, 1024], P('mode', None, 'row'), may hold values from -8 to 8
- backward_second: bfloat16 [64, 2, 1024, 1024], P('mode', None, 'row'), may hold values from -8 to 8
- phase_first: float32 [1024, 1024], P('row'), may hold values from -3.140625 to 3.140625
- phase_second: float32 [1024, 1024], P('row'), may hold values from -3.140625 to 3.140625
Outputs:
- mask_first: bfloat16 [2, 1024, 1024], P(None, 'row')
- mask_second: bfloat16 [2, 1024, 1024], P(None, 'row')
- arrived: bfloat16 [64, 2, 1024, 1024], P('mode', None, 'row')
All inputs are finite; a program needn't handle non-finite values.
Results may differ from a plain program's by a relative error of at most 0.03.
Values may be sent and summed in bfloat16 or wider, within the bound.
A program may use at most 64 MiB of HBM per device.

v0:
```python
import math

import jax
import jax.numpy as jnp
from jax import lax
from jax.sharding import PartitionSpec as P

GRID = 1024


def make_tables(grid_size):
    indices = jnp.arange(grid_size, dtype=jnp.int32)
    turns = indices[:, None] * indices[None, :] % grid_size
    angles = turns.astype(jnp.float32) * (2.0 * math.pi / grid_size)
    cosine = jnp.cos(angles).astype(jnp.bfloat16)
    sine_table = jnp.sin(angles).astype(jnp.bfloat16)
    frequency = (indices + grid_size // 2) % grid_size - grid_size // 2
    phases = (frequency * frequency % (2 * grid_size)).astype(jnp.float32) * (math.pi / grid_size)
    return (cosine, sine_table, jnp.cos(phases), -jnp.sin(phases))


def transform(field, tables, direct, along_rows):
    cosine, sine_table, chirp_real, chirp_imag = tables
    if along_rows:
        with_cos = jnp.einsum("uk,mpkc->mpuc", cosine, field, preferred_element_type=jnp.float32)
        with_sin = jnp.einsum(
            "uk,mpkc->mpuc", sine_table, field, preferred_element_type=jnp.float32
        )
        factor_real = chirp_real[:, None]
        factor_imag = chirp_imag[:, None]
    else:
        with_cos = jnp.einsum("mpru,uk->mprk", field, cosine, preferred_element_type=jnp.float32)
        with_sin = jnp.einsum(
            "mpru,uk->mprk", field, sine_table, preferred_element_type=jnp.float32
        )
        factor_real = chirp_real
        factor_imag = chirp_imag
    if direct:
        part_real = with_cos[:, 0] + with_sin[:, 1]
        part_imag = with_cos[:, 1] - with_sin[:, 0]
        out_real = part_real * factor_real - part_imag * factor_imag
        out_imag = part_real * factor_imag + part_imag * factor_real
    else:
        length = cosine.shape[0]
        out_real = (with_cos[:, 0] - with_sin[:, 1]) / length
        out_imag = (with_cos[:, 1] + with_sin[:, 0]) / length
    return jnp.stack([out_real, out_imag], axis=1).astype(jnp.bfloat16)


def new_mask(front, back, phase):
    front_real = front[:, 0].astype(jnp.float32)
    front_imag = front[:, 1].astype(jnp.float32)
    back_real = back[:, 0].astype(jnp.float32)
    back_imag = back[:, 1].astype(jnp.float32)
    prod_real = back_real * front_real + back_imag * front_imag
    prod_imag = back_real * front_imag - back_imag * front_real
    cos_phase = jnp.cos(phase)
    sin_phase = jnp.sin(phase)
    local_real = jnp.sum(prod_real * cos_phase - prod_imag * sin_phase, axis=(1, 2))
    local_imag = jnp.sum(prod_real * sin_phase + prod_imag * cos_phase, axis=(1, 2))
    over_real, over_imag = lax.psum((local_real, local_imag), "row")
    plane_cols = phase.shape[1]
    total_real = (
        jnp.sum(over_real[:, None, None] * prod_real + over_imag[:, None, None] * prod_imag, axis=0)
        / plane_cols
    )
    total_imag = (
        jnp.sum(over_real[:, None, None] * prod_imag - over_imag[:, None, None] * prod_real, axis=0)
        / plane_cols
    )
    total_real, total_imag = lax.psum((total_real, total_imag), "mode")
    magnitude = total_real * total_real + total_imag * total_imag
    power_total = lax.psum(jnp.sum(magnitude), "row")
    scale_factor = lax.rsqrt(magnitude + 0.25 * (power_total / (plane_cols * plane_cols)) + 1e-06)
    return jnp.stack([total_real * scale_factor, -total_imag * scale_factor]).astype(jnp.bfloat16)


def on_device(forward, backward_first, backward_second, phase_first, phase_second):
    tables = make_tables(GRID)
    mask_first = new_mask(forward, backward_first, phase_first)
    mask_real = mask_first[0].astype(jnp.float32)
    mask_imag = mask_first[1].astype(jnp.float32)
    front_real = forward[:, 0].astype(jnp.float32)
    front_imag = forward[:, 1].astype(jnp.float32)
    field = jnp.stack(
        [
            front_real * mask_real - front_imag * mask_imag,
            front_real * mask_imag + front_imag * mask_real,
        ],
        axis=1,
    ).astype(jnp.bfloat16)
    field = transform(field, tables, True, False)
    field = transform(field, tables, False, False)
    spectrum = transform(
        lax.all_to_all(field, "row", split_axis=3, concat_axis=2, tiled=True), tables, True, True
    )
    spectrum = transform(spectrum, tables, False, True)
    arrived = lax.all_to_all(spectrum, "row", split_axis=2, concat_axis=3, tiled=True)
    mask_second = new_mask(arrived, backward_second, phase_second)
    return (mask_first, mask_second, arrived)


def solution(mesh):
    in_specs = (
        P("mode", None, "row", None),
        P("mode", None, "row", None),
        P("mode", None, "row", None),
        P("row", None),
        P("row", None),
    )
    out_specs = (P(None, "row", None), P(None, "row", None), P("mode", None, "row", None))
    return jax.shard_map(
        on_device, mesh=mesh, in_specs=in_specs, out_specs=out_specs, check_vma=False
    )
```

profile of v0, /device:TPU:1, one launch (start us, length us, event | category | flops | bytes accessed | tf_op | source)
XLA Modules:
  0.0 2020.7 jit_solution(8844797479237298810)
XLA Ops:
  7.2 0.0 copy-start
  7.2 0.0 copy-start.7
  7.2 0.0 all-reduce.9.cloned.1.call-start
  7.2 2.9 fusion.137
  10.1 0.0 copy-done
  10.1 0.0 copy-done.7
  10.1 1.0 subtract_reduce_fusion.1
  11.2 47.2 %all-reduce.3 = (f32[]{:T(128)}, f32[]{:T(128)}) all-reduce(f32[]{:T(128)} %get-tuple-element.6, f32[]{:T(128)} %get-tuple-element.5), channel_id=1, replica_groups=mesh['mode'=64,'row'=8] {'row'}, use_global_device_ids=true, to_apply=%region_3.4 | all-reduce | flops 2 | bytes 16 | tf_op jit(solution)/shard_map/psum | solution.py:61
  58.3 2.4 add_multiply_fusion.1
  60.8 0.0 all-reduce.9.cloned.1.call-update
  60.8 825.1 %all-reduce.9.cloned.1.call-done = (f32[128,1024]{1,0:T(8,128)}, f32[128,1024]{1,0:T(8,128)}) async-done(((f32[128,1024]{1,0:T(8,128)}, f32[128,1024]{1,0:T(8,128)}), (f32[128,1024]{1,0:T(8,128)}, f32[128,1024]{1,0:T(8,128)})) %all-reduce.9.cloned.1.call-update) | async-done | bytes 1048592 | tf_op jit(solution)/shard_map/psum | solution.py:71
  885.8 0.0 copy-start.1
  885.8 0.0 copy-start.2
  885.8 2.0 fusion.72
  887.9 0.1 sine_negate_fusion
  887.9 35.8 %psum.74 = f32[]{:T(128)} all-reduce(f32[]{:T(128)} %fusion.72), channel_id=1, replica_groups=mesh['mode'=64,'row'=8] {'row'}, use_global_device_ids=true, to_apply=%region_7.8 | all-reduce | flops 1 | bytes 8 | tf_op jit(solution)/shard_map/psum | solution.py:73
  924.4 0.0 copy-done.1
  924.4 0.0 copy-done.2
  924.4 0.3 fusion.57
  924.7 0.2 fusion.59
  924.8 16.1 fusion.36
  941.0 15.8 fusion.24
  956.8 0.2 fusion.76
  957.0 16.4 fusion.39
  973.4 15.8 fusion.27
  989.2 0.2 fusion.71
  989.4 0.1 pad_maximum_fusion.3
  989.5 0.4 copy.10
  989.9 24.8 %all_to_all.33 = bf16[1,2,128,1024]{2,1,0,3:T(2,128)(2,1)S(1)} all-to-all(bf16[1,2,128,1024]{2,1,0,3:T(2,128)(2,1)S(1)} %copy.10), channel_id=1, replica_groups=mesh['mode'=64,'row'=8] {'row'}, dimensions={3} | all-to-all | bytes 1048576 | tf_op jit(solution)/shard_map/all_to_all | solution.py:95
  1014.7 0.3 copy.17
  1015.1 0.2 reshape.507
  1015.3 16.3 fusion.42
  1031.7 16.6 fusion.30
  1048.3 0.2 fusion.78
  1048.5 16.0 fusion.45
  1064.5 15.9 fusion.33
  1080.4 0.2 fusion.67
  1080.6 0.1 pad_maximum_fusion.5
  1080.6 0.0 copy-start.6
  1080.6 1.1 copy.12
  1081.8 3.5 all-to-all-start.1
  1085.3 0.0 all-reduce.7.cloned.1.call-start
  1085.3 0.0 copy-done.6
  1085.3 1.9 fusion.136
  1087.2 13.8 all-to-all-done.1
  1101.0 0.3 copy.16
  1101.4 0.2 all_to_all.30
  1101.6 0.0 copy-start.5
  1101.6 2.1 subtract_reduce_fusion
  1103.8 0.0 copy-done.5
  1103.8 32.4 %all-reduce.2 = (f32[]{:T(128)}, f32[]{:T(128)}) all-reduce(f32[]{:T(128)} %get-tuple-element.4, f32[]{:T(128)} %get-tuple-element.3), channel_id=1, replica_groups=mesh['mode'=64,'row'=8] {'row'}, use_global_device_ids=true, to_apply=%region_11.12 | all-reduce | flops 2 | bytes 16 | tf_op jit(solution)/shard_map/psum | solution.py:61
  1136.2 2.4 add_multiply_fusion
  1138.6 0.0 all-reduce.7.cloned.1.call-update
  1138.6 834.5 %all-reduce.7.cloned.1.call-done = (f32[128,1024]{1,0:T(8,128)}, f32[128,1024]{1,0:T(8,128)}) async-done(((f32[128,1024]{1,0:T(8,128)}, f32[128,1024]{1,0:T(8,128)}), (f32[128,1024]{1,0:T(8,128)}, f32[128,1024]{1,0:T(8,128)})) %all-reduce.7.cloned.1.call-update) | async-done | bytes 1048592 | tf_op jit(solution)/shard_map/psum | solution.py:71
  1973.1 0.0 copy-start.3
  1973.1 0.0 copy-start.4
  1973.1 2.0 fusion.73
  1975.2 0.8 pad_maximum_fusion
  1976.0 35.7 %psum.79 = f32[]{:T(128)} all-reduce(f32[]{:T(128)} %fusion.73), channel_id=1, replica_groups=mesh['mode'=64,'row'=8] {'row'}, use_global_device_ids=true, to_apply=%region_15.16 | all-reduce | flops 1 | bytes 8 | tf_op jit(solution)/shard_map/psum | solution.py:73
  2012.4 0.0 copy-done.3
  2012.4 0.0 copy-done.4
  2012.4 0.2 fusion.80
  2012.6 0.8 pad_maximum_fusion.6
Async XLA Ops:
  7.2 2.9 copy-start
  7.2 2.9 copy-start.7
  7.2 878.7 %all-reduce.9.cloned.1.call-start = ((), (), s32[]{:S(2)}) async-start(), calls=%async_computation.3 | async-start | bytes 2097152 | tf_op jit(solution)/shard_map/psum | solution.py:71
  885.8 38.5 %copy-start.1 = (f32[128,1024]{1,0:T(8,128)S(1)}, f32[128,1024]{1,0:T(8,128)}, u32[]{:S(2)}) copy-start(f32[128,1024]{1,0:T(8,128)} %get-tuple-element.9) | copy-start | bytes 1572868
  885.8 38.5 %copy-start.2 = (f32[128,1024]{1,0:T(8,128)S(1)}, f32[128,1024]{1,0:T(8,128)}, u32[]{:S(2)}) copy-start(f32[128,1024]{1,0:T(8,128)} %get-tuple-element.10) | copy-start | bytes 1572868
  1080.6 4.7 copy-start.6
  1081.8 19.3 all-to-all-start.1
  1085.3 887.9 %all-reduce.7.cloned.1.call-start = ((), (), s32[]{:S(2)}) async-start(), calls=%async_computation.2 | async-start | bytes 2097152 | tf_op jit(solution)/shard_map/psum | solution.py:71
  1101.6 2.2 copy-start.5
  1973.1 39.3 %copy-start.3 = (f32[128,1024]{1,0:T(8,128)S(1)}, f32[128,1024]{1,0:T(8,128)}, u32[]{:S(2)}) copy-start(f32[128,1024]{1,0:T(8,128)} %get-tuple-element.7) | copy-start | bytes 1572868
  1973.1 39.3 %copy-start.4 = (f32[128,1024]{1,0:T(8,128)S(1)}, f32[128,1024]{1,0:T(8,128)}, u32[]{:S(2)}) copy-start(f32[128,1024]{1,0:T(8,128)} %get-tuple-element.8) | copy-start | bytes 1572868
Sparse Core Ops, SparseCore 0:
  60.9 824.8 all-reduce.8
  1138.7 834.3 all-reduce.6
where the time goes:
time: 2040 us; the launch traced here: 2020 us
  waiting for transfers between devices  1670 us (82%)
  blocking collectives  176 us (9%)
  matrix products  129 us (6%)
    psum x2, waiting for transfers between devices, new_mask(): total_real, total_imag = lax.psum((total_real, total_imag), 'mode')  1660 us
    psum x2, blocking collectives, new_mask(): over_real, over_imag = lax.psum((local_real, local_imag), 'row')  79.6 us
    psum x2, blocking collectives, new_mask(): power_total = lax.psum(jnp.sum(magnitude), 'row')  71.5 us
  transfers between devices with their start and end apart: 3, of which 3 were waited for; matrix products, arithmetic and copies ran while one was open for 0% of the time, Pallas kernels for 0%

commit v1 on v0

v1 whole, which is shorter than its diff:
```python
import functools
import math

import jax
import jax.numpy as jnp
import ml_dtypes
import numpy as np
from jax import lax
from jax.experimental import pallas as pl
from jax.experimental.pallas import tpu as pltpu
from jax.sharding import PartitionSpec as P

GRID = 1024
ROWS = 128
MESH = pl.DeviceIdType.MESH
F32 = jnp.float32
BF16 = jnp.bfloat16


@functools.cache
def propagator():
    u = np.arange(GRID)
    turns = u[:, None] * u[None, :] % GRID
    angles = np.minimum(turns, GRID - turns) * (2.0 * math.pi / GRID)
    sign = np.where(turns <= GRID // 2, 1.0, -1.0)
    cosine = np.cos(angles).astype(ml_dtypes.bfloat16).astype(np.float64)
    sine = (sign * np.sin(angles)).astype(ml_dtypes.bfloat16).astype(np.float64)
    f = (u + GRID // 2) % GRID - GRID // 2
    phases = (f * f % (2 * GRID)) * (math.pi / GRID)
    chirp = np.cos(phases) - 1j * np.sin(phases)
    h = ((cosine - 1j * sine) * chirp) @ (cosine + 1j * sine) / GRID
    return np.stack([h.real, h.imag]).astype(ml_dtypes.bfloat16)


def cos_sin(phase):
    x = phase * 0.5
    z = x * x
    s = [(-1.0) ** i / math.factorial(2 * i + 1) for i in range(7)]
    c = [(-1.0) ** i / math.factorial(2 * i) for i in range(7)]
    ps = jnp.full_like(z, s[-1])
    for v in s[-2::-1]:
        ps = ps * z + v
    pc = jnp.full_like(z, c[-1])
    for v in c[-2::-1]:
        pc = pc * z + v
    sn = ps * x
    return 1.0 - 2.0 * sn * sn, 2.0 * sn * pc


def fold(v):
    tiles = [
        v[r : r + 8, c : c + 128] for r in range(0, v.shape[0], 8) for c in range(0, v.shape[1], 128)
    ]
    while len(tiles) > 1:
        tiles = [sum(tiles[i : i + 2]) for i in range(0, len(tiles), 2)]
    return tiles[0]


def kernel(
    f_in, b1_in, b2_in, p1_in, p2_in, h_in, m1_out, m2_out, a_out,
    f, b, ph, h, prod, raw, irecv, wrecv, part, zrecv, full, precv, mask, s, t, g, y, arr,
    ls, ss, rs,
):
    mode = lax.axis_index("mode")
    row = lax.axis_index("row")
    zl = mode // 8
    yc = lax.rem(mode, 8)

    def row_peer(k):
        return (mode, lax.rem(row + k, 8))

    def yc_peer(k):
        return (zl * 8 + lax.rem(yc + k, 8), row)

    def z_peer(k):
        return (lax.rem(zl + k, 8) * 8 + yc, row)

    bar = pltpu.get_barrier_semaphore()

    def greet(k, _):
        for p in (row_peer(k), yc_peer(k), z_peer(k)):
            pl.semaphore_signal(bar, inc=1, device_id=p, device_id_type=MESH)
        return 0

    lax.fori_loop(1, 8, greet, 0)

    loads = [
        pltpu.make_async_copy(src, dst, ls.at[i])
        for i, (src, dst) in enumerate(
            [(f_in, f), (b1_in, b.at[0]), (p1_in, ph.at[0]), (h_in, h), (b2_in, b.at[1]), (p2_in, ph.at[1])]
        )
    ]
    for c in loads:
        c.start()

    class Stage:
        def __init__(self, n, src, dst, peer):
            self.n, self.src, self.dst, self.peer = n, src, dst, peer

        def desc(self, k):
            return pltpu.make_async_remote_copy(
                src_ref=self.src(k), dst_ref=self.dst(k), send_sem=ss.at[self.n, k],
                recv_sem=rs.at[self.n, k], device_id=self.peer(k), device_id_type=MESH,
            )

        def loop(self, what):
            def body(k, _):
                what(self.desc(k))
                return 0

            lax.fori_loop(1, 8, body, 0)

        def start(self):
            self.loop(lambda d: d.start())

        def recv(self):
            self.loop(lambda d: d.wait_recv())

        def sent(self):
            self.loop(lambda d: d.wait_send())

    stages = []

    def stage(*args):
        stages.append(Stage(len(stages), *args))
        return stages[-1]

    def new_mask(i, front, first):
        back, phase = b.at[i], ph.at[i]

        def products(j, acc):
            rows = pl.ds(pl.multiple_of(j * 16, 16), 16)
            fr, fi = front[0, rows, :].astype(F32), front[1, rows, :].astype(F32)
            br, bi = back[0, rows, :].astype(F32), back[1, rows, :].astype(F32)
            pr = br * fr + bi * fi
            pi = br * fi - bi * fr
            prod[i, j, 0] = pr.astype(BF16)
            prod[i, j, 1] = pi.astype(BF16)
            c, sn = cos_sin(phase[rows, :])
            return acc[0] + fold(pr * c - pi * sn), acc[1] + fold(pr * sn + pi * c)

        zero = jnp.zeros((8, 128), F32)
        ir, ii = lax.fori_loop(0, 8, products, (zero, zero))
        irecv[i, 0, 0] = ir
        irecv[i, 0, 1] = ii
        if first:
            pl.semaphore_wait(bar, 21)
        over = stage(lambda k: irecv.at[i, 0], lambda k: irecv.at[i, k], row_peer)
        over.start()
        share = stage(lambda k: prod.at[i, lax.rem(yc + k, 8)], lambda k: raw.at[i, k], yc_peer)
        share.start()
        over.recv()
        for q in range(2):
            wrecv[i, 0, q] = sum(irecv[i, k, q] for k in range(8))
        weight = stage(lambda k: wrecv.at[i, 0], lambda k: wrecv.at[i, k], yc_peer)
        weight.start()
        raw[i, 0] = prod[i, yc]
        share.recv()
        weight.recv()

        def weighted(k, acc):
            wr = jnp.sum(wrecv[i, k, 0], axis=(0, 1), keepdims=True) * (1.0 / GRID)
            wi = jnp.sum(wrecv[i, k, 1], axis=(0, 1), keepdims=True) * (1.0 / GRID)
            pr, pi = raw[i, k, 0].astype(F32), raw[i, k, 1].astype(F32)
            return acc[0] + (wr * pr + wi * pi), acc[1] + (wr * pi - wi * pr)

        zero = jnp.zeros((16, GRID), F32)
        tr, ti = lax.fori_loop(0, 8, weighted, (zero, zero))
        for q in range(8):
            part[i, q, 0] = tr[:, q * 128 : q * 128 + 128].astype(BF16)
            part[i, q, 1] = ti[:, q * 128 : q * 128 + 128].astype(BF16)
        scatter = stage(lambda k: part.at[i, lax.rem(zl + k, 8)], lambda k: zrecv.at[i, k], z_peer)
        scatter.start()
        zrecv[i, 0] = part[i, zl]
        scatter.recv()
        full[i, yc, zl] = sum(zrecv[i, k].astype(F32) for k in range(8)).astype(BF16)
        gather_z = stage(lambda k: full.at[i, yc, zl], lambda k: full.at[i, yc, zl], z_peer)
        gather_z.start()
        gather_z.recv()
        gather_yc = stage(lambda k: full.at[i, yc], lambda k: full.at[i, yc], yc_peer)
        gather_yc.start()
        gather_yc.recv()

        def power(j, acc):
            for q in range(8):
                v = full[i, j, q].astype(F32)
                acc = acc + fold(v[0] * v[0] + v[1] * v[1])
            return acc

        precv[i, 0] = lax.fori_loop(0, 8, power, jnp.zeros((8, 128), F32))
        powers = stage(lambda k: precv.at[i, 0], lambda k: precv.at[i, k], row_peer)
        powers.start()
        powers.recv()
        total = sum(precv[i, k] for k in range(8))
        mean = jnp.sum(total, axis=(0, 1), keepdims=True) * (1.0 / (GRID * GRID))
        floor = 0.25 * mean + 1e-6

        def finish(j, _):
            rows = pl.ds(pl.multiple_of(j * 16, 16), 16)
            for q in range(8):
                v = full[i, j, q].astype(F32)
                scale = lax.rsqrt(v[0] * v[0] + v[1] * v[1] + floor)
                mask[i, 0, rows, q * 128 : q * 128 + 128] = (v[0] * scale).astype(BF16)
                mask[i, 1, rows, q * 128 : q * 128 + 128] = (-v[1] * scale).astype(BF16)
            return 0

        lax.fori_loop(0, 8, finish, 0)

    for c in loads[:3]:
        c.wait()
    new_mask(0, f, True)
    outs = [pltpu.make_async_copy(mask.at[0], m1_out, ls.at[6])]
    outs[0].start()

    def apply(j, _):
        rows = pl.ds(pl.multiple_of(j * 16, 16), 16)
        fr, fi = f[0, rows, :].astype(F32), f[1, rows, :].astype(F32)
        mr, mi = mask[0, 0, rows, :].astype(F32), mask[0, 1, rows, :].astype(F32)
        s[rows, :] = (fr * mr - fi * mi).astype(BF16)
        s[pl.ds(pl.multiple_of(ROWS + j * 16, 16), 16), :] = (fr * mi + fi * mr).astype(BF16)
        return 0

    lax.fori_loop(0, 8, apply, 0)
    for c in loads[3:]:
        c.wait()

    to_cols = stage(
        lambda k: t.at[:, pl.ds(pl.multiple_of(lax.rem(row + k, 8) * 256, 256), 256)],
        lambda k: g.at[pl.ds(pl.multiple_of(row * ROWS, ROWS), ROWS), :],
        row_peer,
    )
    far = 2 * (1 - row // 4)

    def send_to(st, p):
        @pl.when(p != row)
        def _():
            st.desc(lax.rem(p - row + 8, 8)).start()

    def columns(j, _):
        n = lax.rem(far + j, 4)
        cols = pl.ds(pl.multiple_of(n * 256, 256), 256)
        a = jnp.dot(s[...], h[0, :, cols], preferred_element_type=F32)
        c = jnp.dot(s[...], h[1, :, cols], preferred_element_type=F32)
        tr = (a[:ROWS] - c[ROWS:]).astype(BF16)
        ti = (c[:ROWS] + a[ROWS:]).astype(BF16)
        for e in range(2):
            at = n * 512 + e * 256
            t[:, pl.ds(pl.multiple_of(at, 128), 128)] = tr[:, e * 128 : e * 128 + 128]
            t[:, pl.ds(pl.multiple_of(at + 128, 128), 128)] = ti[:, e * 128 : e * 128 + 128]
        for e in range(2):
            send_to(to_cols, 2 * n + e)
        return 0

    lax.fori_loop(0, 4, columns, 0)
    g[pl.ds(pl.multiple_of(row * ROWS, ROWS), ROWS), :] = t[
        :, pl.ds(pl.multiple_of(row * 256, 256), 256)
    ]
    to_cols.recv()

    to_rows = stage(
        lambda k: y.at[lax.rem(row + k, 8)],
        lambda k: arr.at[:, :, pl.ds(pl.multiple_of(row * 128, 128), 128)],
        row_peer,
    )

    def rows_(j, _):
        n = lax.rem(far + j, 4)
        rows = pl.ds(pl.multiple_of(n * 256, 256), 256)
        a = jnp.dot(h[0, rows, :], g[...], preferred_element_type=F32)
        c = jnp.dot(h[1, rows, :], g[...], preferred_element_type=F32)
        yr = (a[:, :128] - c[:, 128:]).astype(BF16)
        yi = (a[:, 128:] + c[:, :128]).astype(BF16)
        for e in range(2):
            y[2 * n + e, 0] = yr[e * ROWS : e * ROWS + ROWS]
            y[2 * n + e, 1] = yi[e * ROWS : e * ROWS + ROWS]
        for e in range(2):
            send_to(to_rows, 2 * n + e)
        return 0

    lax.fori_loop(0, 4, rows_, 0)
    arr[:, :, pl.ds(pl.multiple_of(row * 128, 128), 128)] = y[row]
    to_rows.recv()
    outs.append(pltpu.make_async_copy(arr, a_out, ls.at[7]))
    outs[1].start()
    new_mask(1, arr, False)
    outs.append(pltpu.make_async_copy(mask.at[1], m2_out, ls.at[8]))
    outs[2].start()
    for st in stages:
        st.sent()
    for c in outs:
        c.wait()


def on_device(forward, backward_first, backward_second, phase_first, phase_second):
    hbm = pl.BlockSpec(memory_space=pl.ANY)
    block = (2, ROWS, GRID)
    m1, m2, arrived = pl.pallas_call(
        kernel,
        out_shape=[jax.ShapeDtypeStruct(block, BF16)] * 3,
        in_specs=[hbm] * 6,
        out_specs=[hbm] * 3,
        scratch_shapes=[
            pltpu.VMEM(block, BF16),
            pltpu.VMEM((2, *block), BF16),
            pltpu.VMEM((2, ROWS, GRID), F32),
            pltpu.VMEM((2, GRID, GRID), BF16),
            pltpu.VMEM((2, 8, 2, 16, GRID), BF16),
            pltpu.VMEM((2, 8, 2, 16, GRID), BF16),
            pltpu.VMEM((2, 8, 2, 8, 128), F32),
            pltpu.VMEM((2, 8, 2, 8, 128), F32),
            pltpu.VMEM((2, 8, 2, 16, 128), BF16),
            pltpu.VMEM((2, 8, 2, 16, 128), BF16),
            pltpu.VMEM((2, 8, 8, 2, 16, 128), BF16),
            pltpu.VMEM((2, 8, 8, 128), F32),
            pltpu.VMEM((2, *block), BF16),
            pltpu.VMEM((2 * ROWS, GRID), BF16),
            pltpu.VMEM((ROWS, 2 * GRID), BF16),
            pltpu.VMEM((GRID, 256), BF16),
            pltpu.VMEM((8, 2, ROWS, 128), BF16),
            pltpu.VMEM(block, BF16),
            pltpu.SemaphoreType.DMA((9,)),
            pltpu.SemaphoreType.DMA((16, 8)),
            pltpu.SemaphoreType.DMA((16, 8)),
        ],
        compiler_params=pltpu.CompilerParams(
            collective_id=0, has_side_effects=True, vmem_limit_bytes=40 * 2**20
        ),
    )(
        forward[0], backward_first[0], backward_second[0], phase_first, phase_second,
        jnp.asarray(propagator()),
    )
    return m1, m2, arrived[None]


def solution(mesh):
    in_specs = (
        P("mode", None, "row", None),
        P("mode", None, "row", None),
        P("mode", None, "row", None),
        P("row", None),
        P("row", None),
    )
    out_specs = (P(None, "row", None), P(None, "row", None), P("mode", None, "row", None))
    return jax.shard_map(
        on_device, mesh=mesh, in_specs=in_specs, out_specs=out_specs, check_vma=False
    )
```

time: 2040 us -> 173 us (0.08)
  waiting for transfers between devices: 1670 us -> 0 us
  blocking collectives: 176 us -> 0 us
  Pallas kernels: 0 us -> 162 us
  matrix products: 129 us -> 0 us
    psum x2 -> x0, waiting for transfers between devices: 1660 us -> none  [new_mask(): total_real, total_imag = lax.psum((total_real, total_imag), 'mode')]
    pallas_call x0 -> x1, Pallas kernels: none -> 162 us  [on_device(): pl.pallas_call(kernel, out_shape=[jax.ShapeDtypeStruct(block, BF16)] * 3,...]
    psum x4 -> x0, blocking collectives: 151 us -> none  [the longest x2 79.6 us: new_mask(): over_real, over_imag = lax.psum((local_real, local_imag), 'row')]
    dot_general x8 -> x0, matrix products: 129 us -> none  [the longest x2 32.5 us: transform(): jnp.einsum('mpru,uk->mprk', field, sine_table, preferred_element_type=jnp...]
    all_to_all x1 -> x0, blocking collectives: 24.8 us -> none  [on_device(): lax.all_to_all(field, 'row', split_axis=3, concat_axis=2, tiled=True)]
  transfers between devices with their start and end apart: 3 -> 0, of which waited for: 3 -> 0; matrix products, arithmetic and copies ran while one was open for 0% -> 0% of each run, Pallas kernels for 0% -> 0%
where the time goes in v1:
time: 173 us; the launch traced here: 172 us
  Pallas kernels  162 us (94%)
  local copies, waits for them, and re-layouts  9.77 us (6%)
    pallas_call x1, Pallas kernels, on_device(): pl.pallas_call(kernel, out_shape=[jax.ShapeDtypeStruct(block, BF16)] * 3,...  162 us
    unnamed x15, local copies, waits for them, and re-layouts  9.77 us

profile of v1, /device:TPU:1, one launch (start us, length us, event | category | flops | bytes accessed | tf_op | source)
XLA Modules:
  0.0 172.3 jit_solution(14918691467066208310)
XLA Ops:
  0.6 0.0 copy-start
  0.6 2.2 %copy-done = bf16[2,1024,1024]{2,1,0:T(8,128)(2,1)S(1)} copy-done((bf16[2,1024,1024]{2,1,0:T(8,128)(2,1)S(1)}, bf16[2,1024,1024]{2,1,0:T(8,128)(2,1)}, u32[]{:S(2)}) %copy-start) | copy-done | bytes 4194328
  2.8 0.0 copy-start.1
  2.8 1.0 copy-done.1
  3.9 0.0 copy-start.2
  3.9 1.0 copy-done.2
  4.9 0.0 copy-start.3
  4.9 1.0 copy-done.3
  5.9 0.0 copy-start.4
  6.0 1.0 copy-done.4
  7.0 0.0 copy-start.5
  7.0 1.0 copy-done.5
  8.0 161.8 %shard_map.85 = (bf16[2,128,1024]{2,1,0:T(8,128)(2,1)S(1)}, bf16[2,128,1024]{2,1,0:T(8,128)(2,1)S(1)}, bf16[2,128,1024]{2,1,0:T(8,128)(2,1)S(1)}) custom-call(bf16[2,128,1024]{2,1,0:T(8,128)(2,1)S(1)} %bitcast.5, bf16[2,128,1024]{2,1,0:T(8,128)(2,1)S(1)} %bitcast.6, bf16[2,128,1024]{2,1,0:T(8,128)(2,1)S(1)} %bitcast.7, f32[128,1024]{1,0:T(8,128)S(1)} %copy-done.4, ...), custom_call_target="tpu_custom_call" | custom-call | tf_op jit(solution)/shard_map/pallas_call | solution.py:297
  169.9 0.8 copy.12
  170.7 0.8 copy.13
  171.5 0.8 copy.14
Async XLA Ops:
  0.6 2.2 %copy-start = (bf16[2,1024,1024]{2,1,0:T(8,128)(2,1)S(1)}, bf16[2,1024,1024]{2,1,0:T(8,128)(2,1)}, u32[]{:S(2)}) copy-start(bf16[2,1024,1024]{2,1,0:T(8,128)(2,1)} %constant.2.clone.h_in) | copy-start | bytes 12582916
  2.8 1.0 copy-start.1
  3.9 1.0 copy-start.2
  4.9 1.0 copy-start.3
  5.9 1.0 copy-start.4
  7.0 1.0 copy-start.5

commit v2 on v1

--- a/solution.py
+++ b/solution.py
@@ -58,7 +58,7 @@
 
 def kernel(
     f_in, b1_in, b2_in, p1_in, p2_in, h_in, m1_out, m2_out, a_out,
-    f, b, ph, h, prod, raw, irecv, wrecv, part, zrecv, full, precv, mask, s, t, g, y, arr,
+    f, b, ph, h, prod, raw, irecv, wrecv, part, zrecv, full, precv, prow, mask, s, t, g, y, arr,
     ls, ss, rs,
 ):
     mode = lax.axis_index("mode")
@@ -75,14 +75,34 @@
     def z_peer(k):
         return (lax.rem(zl + k, 8) * 8 + yc, row)
 
+    def z16_peer(k):
+        z = lax.rem((row // 4) * 8 + zl + k, 16)
+        return (lax.rem(z, 8) * 8 + yc, (z // 8) * 4 + lax.rem(row, 4))
+
+    def y_peer(k):
+        return (zl * 8 + lax.rem(yc + 2 * (k // 8), 8), row)
+
+    def c_peer(k):
+        return (mode + 1 - 2 * lax.rem(mode, 2), row)
+
+    def xyc_peer(k):
+        at = lax.rem(lax.rem(row, 4) * 8 + yc + k, 32)
+        return (zl * 8 + lax.rem(at, 8), (row // 4) * 4 + at // 8)
+
     bar = pltpu.get_barrier_semaphore()
-
-    def greet(k, _):
-        for p in (row_peer(k), yc_peer(k), z_peer(k)):
-            pl.semaphore_signal(bar, inc=1, device_id=p, device_id_type=MESH)
-        return 0
-
-    lax.fori_loop(1, 8, greet, 0)
+    n_greet = 0
+
+    def greet(first, last, peer):
+        def body(k, _):
+            pl.semaphore_signal(bar, inc=1, device_id=peer(k), device_id_type=MESH)
+            return 0
+
+        lax.fori_loop(first, last, body, 0)
+        return last - first
+
+    n_greet += greet(1, 8, row_peer)
+    n_greet += greet(1, 16, z16_peer)
+    n_greet += greet(1, 32, xyc_peer)
 
     loads = [
         pltpu.make_async_copy(src, dst, ls.at[i])
@@ -94,13 +114,15 @@
         c.start()
 
     class Stage:
-        def __init__(self, n, src, dst, peer):
-            self.n, self.src, self.dst, self.peer = n, src, dst, peer
+        def __init__(self, n, hi, src, dst, peer, slot=None):
+            self.n, self.hi, self.src, self.dst, self.peer = n, hi, src, dst, peer
+            self.slot = slot or (lambda k: k)
+            self.lo = 8 if peer is y_peer else 1
 
         def desc(self, k):
             return pltpu.make_async_remote_copy(
                 src_ref=self.src(k), dst_ref=self.dst(k), send_sem=ss.at[self.n, k],
-                recv_sem=rs.at[self.n, k], device_id=self.peer(k), device_id_type=MESH,
+                recv_sem=rs.at[self.n, self.slot(k)], device_id=self.peer(k), device_id_type=MESH,
             )
 
         def loop(self, what):
@@ -108,7 +130,7 @@
                 what(self.desc(k))
                 return 0
 
-            lax.fori_loop(1, 8, body, 0)
+            lax.fori_loop(self.lo, self.hi, body, 0)
 
         def start(self):
             self.loop(lambda d: d.start())
@@ -134,66 +156,116 @@
             br, bi = back[0, rows, :].astype(F32), back[1, rows, :].astype(F32)
             pr = br * fr + bi * fi
             pi = br * fi - bi * fr
-            prod[i, j, 0] = pr.astype(BF16)
-            prod[i, j, 1] = pi.astype(BF16)
+            for q in range(8):
+                prod[i, j, q, 0] = pr[:, q * 128 : q * 128 + 128].astype(BF16)
+                prod[i, j, q, 1] = pi[:, q * 128 : q * 128 + 128].astype(BF16)
             c, sn = cos_sin(phase[rows, :])
             return acc[0] + fold(pr * c - pi * sn), acc[1] + fold(pr * sn + pi * c)
 
         zero = jnp.zeros((8, 128), F32)
         ir, ii = lax.fori_loop(0, 8, products, (zero, zero))
-        irecv[i, 0, 0] = ir
-        irecv[i, 0, 1] = ii
+        irecv[i, 0, 0] = jnp.sum(ir, axis=0, keepdims=True)
+        irecv[i, 0, 1] = jnp.sum(ii, axis=0, keepdims=True)
         if first:
-            pl.semaphore_wait(bar, 21)
-        over = stage(lambda k: irecv.at[i, 0], lambda k: irecv.at[i, k], row_peer)
+            pl.semaphore_wait(bar, n_greet)
+        over = stage(8, lambda k: irecv.at[i, 0], lambda k: irecv.at[i, k], row_peer)
         over.start()
-        share = stage(lambda k: prod.at[i, lax.rem(yc + k, 8)], lambda k: raw.at[i, k], yc_peer)
+        share = stage(8, lambda k: prod.at[i, lax.rem(yc + k, 8)], lambda k: raw.at[i, k], yc_peer)
         share.start()
         over.recv()
         for q in range(2):
             wrecv[i, 0, q] = sum(irecv[i, k, q] for k in range(8))
-        weight = stage(lambda k: wrecv.at[i, 0], lambda k: wrecv.at[i, k], yc_peer)
+        weight = stage(8, lambda k: wrecv.at[i, 0], lambda k: wrecv.at[i, k], yc_peer)
         weight.start()
         raw[i, 0] = prod[i, yc]
         share.recv()
         weight.recv()
-
-        def weighted(k, acc):
-            wr = jnp.sum(wrecv[i, k, 0], axis=(0, 1), keepdims=True) * (1.0 / GRID)
-            wi = jnp.sum(wrecv[i, k, 1], axis=(0, 1), keepdims=True) * (1.0 / GRID)
-            pr, pi = raw[i, k, 0].astype(F32), raw[i, k, 1].astype(F32)
-            return acc[0] + (wr * pr + wi * pi), acc[1] + (wr * pi - wi * pr)
-
-        zero = jnp.zeros((16, GRID), F32)
-        tr, ti = lax.fori_loop(0, 8, weighted, (zero, zero))
-        for q in range(8):
-            part[i, q, 0] = tr[:, q * 128 : q * 128 + 128].astype(BF16)
-            part[i, q, 1] = ti[:, q * 128 : q * 128 + 128].astype(BF16)
-        scatter = stage(lambda k: part.at[i, lax.rem(zl + k, 8)], lambda k: zrecv.at[i, k], z_peer)
-        scatter.start()
-        zrecv[i, 0] = part[i, zl]
+        weights = [
+            [jnp.sum(wrecv[i, k, q], axis=1, keepdims=True) * (1.0 / GRID) for q in range(2)]
+            for k in range(8)
+        ]
+
+        scatter = stage(8, lambda k: part.at[i, k], lambda k: zrecv.at[i, k], z_peer)
+
+        def weighted(k, _):
+            q = lax.rem(zl + k, 8)
+            tr = jnp.zeros((16, 128), F32)
+            ti = jnp.zeros((16, 128), F32)
+            for m in range(8):
+                pr, pi = raw[i, m, q, 0].astype(F32), raw[i, m, q, 1].astype(F32)
+                wr, wi = weights[m]
+                tr = tr + (wr * pr + wi * pi)
+                ti = ti + (wr * pi - wi * pr)
+            part[i, k, 0] = tr.astype(BF16)
+            part[i, k, 1] = ti.astype(BF16)
+
+            @pl.when(k < 8)
+            def _():
+                scatter.desc(k).start()
+
+            return 0
+
+        lax.fori_loop(1, 9, weighted, 0)
+        zrecv[i, 0] = part[i, 8]
         scatter.recv()
-        full[i, yc, zl] = sum(zrecv[i, k].astype(F32) for k in range(8)).astype(BF16)
-        gather_z = stage(lambda k: full.at[i, yc, zl], lambda k: full.at[i, yc, zl], z_peer)
+        piece = sum(zrecv[i, k].astype(F32) for k in range(8)).astype(BF16)
+        full[i, yc, zl] = piece
+        gather_z = stage(
+            8, lambda k: full.at[i, yc, zl], lambda k: full.at[i, yc, zl], z_peer, lambda k: zl
+        )
         gather_z.start()
-        gather_z.recv()
-        gather_yc = stage(lambda k: full.at[i, yc], lambda k: full.at[i, yc], yc_peer)
-        gather_yc.start()
-        gather_yc.recv()
-
-        def power(j, acc):
-            for q in range(8):
-                v = full[i, j, q].astype(F32)
-                acc = acc + fold(v[0] * v[0] + v[1] * v[1])
-            return acc
-
-        precv[i, 0] = lax.fori_loop(0, 8, power, jnp.zeros((8, 128), F32))
-        powers = stage(lambda k: precv.at[i, 0], lambda k: precv.at[i, k], row_peer)
-        powers.start()
-        powers.recv()
-        total = sum(precv[i, k] for k in range(8))
-        mean = jnp.sum(total, axis=(0, 1), keepdims=True) * (1.0 / (GRID * GRID))
+        v = piece.astype(F32)
+        precv[i, 0] = jnp.sum(fold(v[0] * v[0] + v[1] * v[1]), axis=0, keepdims=True)
+        power_z = stage(16, lambda k: precv.at[i, 0], lambda k: precv.at[i, k], z16_peer)
+        power_z.start()
+
+        gather_y = stage(32, lambda k: full.at[i, yc, k % 8], lambda k: full.at[i, yc, k % 8], y_peer)
+
+        def onward(q):
+            for o in (1, 2, 3):
+                gather_y.desc(o * 8 + q).start()
+
+        onward(zl)
+
+        def forward_z(d, _):
+            for q in (zl - d, zl + d):
+
+                @pl.when((q >= 0) & (q < 8))
+                def _():
+                    pltpu.make_async_remote_copy(
+                        src_ref=full.at[i, yc, zl], dst_ref=full.at[i, yc, q],
+                        send_sem=ss.at[gather_z.n, 0], recv_sem=rs.at[gather_z.n, q],
+                        device_id=z_peer(1), device_id_type=MESH,
+                    ).wait_recv()
+                    onward(q)
+
+            return 0
+
+        lax.fori_loop(1, 8, forward_z, 0)
+        gather_c = stage(
+            5, lambda k: full.at[i, lax.rem(yc + 2 * k, 8)], lambda k: full.at[i, lax.rem(yc + 2 * k, 8)], c_peer
+        )
+        gather_c.desc(4).start()
+        power_z.recv()
+        prow[i, 0] = sum(precv[i, k] for k in range(16))
+        power_xy = stage(32, lambda k: prow.at[i, 0], lambda k: prow.at[i, k], xyc_peer)
+        power_xy.start()
+
+        def forward_y(o, _):
+            def wait(q, _):
+                gather_y.desc(o * 8 + q).wait_recv()
+                return 0
+
+            lax.fori_loop(0, 8, wait, 0)
+            gather_c.desc(4 - o).start()
+            return 0
+
+        lax.fori_loop(1, 4, forward_y, 0)
+        power_xy.recv()
+        total = sum(prow[i, k] for k in range(32))
+        mean = jnp.sum(total, axis=1, keepdims=True) * (1.0 / (GRID * GRID))
         floor = 0.25 * mean + 1e-6
+        gather_c.recv()
 
         def finish(j, _):
             rows = pl.ds(pl.multiple_of(j * 16, 16), 16)
@@ -205,7 +277,6 @@
             return 0
 
         lax.fori_loop(0, 8, finish, 0)
-
     for c in loads[:3]:
         c.wait()
     new_mask(0, f, True)
@@ -225,6 +296,7 @@
         c.wait()
 
     to_cols = stage(
+        8,
         lambda k: t.at[:, pl.ds(pl.multiple_of(lax.rem(row + k, 8) * 256, 256), 256)],
         lambda k: g.at[pl.ds(pl.multiple_of(row * ROWS, ROWS), ROWS), :],
         row_peer,
@@ -258,6 +330,7 @@
     to_cols.recv()
 
     to_rows = stage(
+        8,
         lambda k: y.at[lax.rem(row + k, 8)],
         lambda k: arr.at[:, :, pl.ds(pl.multiple_of(row * 128, 128), 128)],
         row_peer,
@@ -304,14 +377,15 @@
             pltpu.VMEM((2, *block), BF16),
             pltpu.VMEM((2, ROWS, GRID), F32),
             pltpu.VMEM((2, GRID, GRID), BF16),
-            pltpu.VMEM((2, 8, 2, 16, GRID), BF16),
-            pltpu.VMEM((2, 8, 2, 16, GRID), BF16),
-            pltpu.VMEM((2, 8, 2, 8, 128), F32),
-            pltpu.VMEM((2, 8, 2, 8, 128), F32),
-            pltpu.VMEM((2, 8, 2, 16, 128), BF16),
+            pltpu.VMEM((2, 8, 8, 2, 16, 128), BF16),
+            pltpu.VMEM((2, 8, 8, 2, 16, 128), BF16),
+            pltpu.VMEM((2, 8, 2, 1, 128), F32),
+            pltpu.VMEM((2, 8, 2, 1, 128), F32),
+            pltpu.VMEM((2, 9, 2, 16, 128), BF16),
             pltpu.VMEM((2, 8, 2, 16, 128), BF16),
             pltpu.VMEM((2, 8, 8, 2, 16, 128), BF16),
-            pltpu.VMEM((2, 8, 8, 128), F32),
+            pltpu.VMEM((2, 16, 1, 128), F32),
+            pltpu.VMEM((2, 32, 1, 128), F32),
             pltpu.VMEM((2, *block), BF16),
             pltpu.VMEM((2 * ROWS, GRID), BF16),
             pltpu.VMEM((ROWS, 2 * GRID), BF16),
@@ -319,11 +393,11 @@
             pltpu.VMEM((8, 2, ROWS, 128), BF16),
             pltpu.VMEM(block, BF16),
             pltpu.SemaphoreType.DMA((9,)),
-            pltpu.SemaphoreType.DMA((16, 8)),
-            pltpu.SemaphoreType.DMA((16, 8)),
+            pltpu.SemaphoreType.DMA((20, 32)),
+            pltpu.SemaphoreType.DMA((20, 32)),
         ],
         compiler_params=pltpu.CompilerParams(
-            collective_id=0, has_side_effects=True, vmem_limit_bytes=40 * 2**20
+            collective_id=0, has_side_effects=True, vmem_limit_bytes=60 * 2**20
         ),
     )(
         forward[0], backward_first[0], backward_second[0], phase_first, phase_second,

time: 173 us -> 159 us (0.919)
  Pallas kernels: 162 us -> 152 us
  local copies, waits for them, and re-layouts: 9.77 us -> 5.6 us
    pallas_call x1, Pallas kernels: 162 us -> 152 us  [on_device(): pl.pallas_call(kernel, out_shape=[jax.ShapeDtypeStruct(block, BF16)] * 3,...]
    unnamed x15 -> x3, local copies, waits for them, and re-layouts: 9.77 us -> 5.6 us
where the time goes in v2:
time: 159 us; the launch traced here: 158 us
  Pallas kernels  152 us (96%)
  local copies, waits for them, and re-layouts  5.6 us (4%)
    pallas_call x1, Pallas kernels, on_device(): pl.pallas_call(kernel, out_shape=[jax.ShapeDtypeStruct(block, BF16)] * 3,...  152 us
    unnamed x3, local copies, waits for them, and re-layouts  5.6 us

profile of v2, /device:TPU:1, one launch (start us, length us, event | category | flops | bytes accessed | tf_op | source)
XLA Modules:
  0.0 158.4 jit_solution(12168134722715005432)
XLA Ops:
  0.6 152.1 %shard_map.85 = (bf16[2,128,1024]{2,1,0:T(8,128)(2,1)}, bf16[2,128,1024]{2,1,0:T(8,128)(2,1)}, bf16[2,128,1024]{2,1,0:T(8,128)(2,1)}) custom-call(bf16[2,128,1024]{2,1,0:T(8,128)(2,1)} %bitcast.5, bf16[2,128,1024]{2,1,0:T(8,128)(2,1)} %bitcast.6, bf16[2,128,1024]{2,1,0:T(8,128)(2,1)} %bitcast.7, f32[128,1024]{1,0:T(8,128)} %p1_in.1, f32[128,1024]{1,0:T(8,128)} %p2_in.1, ...), custom_call_target="tpu_custom_call" | custom-call | tf_op jit(solution)/shard_map/pallas_call | solution.py:370
  152.8 1.9 %copy.12 = bf16[2,128,1024]{2,1,0:T(8,128)(2,1)} copy(bf16[2,128,1024]{2,1,0:T(8,128)(2,1)} %get-tuple-element.12) | data formatting | bytes 1048576
  154.6 1.9 %copy.13 = bf16[2,128,1024]{2,1,0:T(8,128)(2,1)} copy(bf16[2,128,1024]{2,1,0:T(8,128)(2,1)} %get-tuple-element.13) | data formatting | bytes 1048576
  156.5 1.9 %copy.14 = bf16[1,2,128,1024]{3,2,1,0:T(8,128)(2,1)} copy(bf16[1,2,128,1024]{3,2,1,0:T(8,128)(2,1)} %bitcast.4) | data formatting | bytes 1048576

commit v3 on v2

v3 whole, which is shorter than its diff:
```python
import functools
import math

import jax
import jax.numpy as jnp
import ml_dtypes
import numpy as np
from jax import lax
from jax.experimental import pallas as pl
from jax.experimental.pallas import tpu as pltpu
from jax.sharding import PartitionSpec as P

GRID = 1024
ROWS = 128
MESH = pl.DeviceIdType.MESH
F32 = jnp.float32
BF16 = jnp.bfloat16


@functools.cache
def propagator():
    u = np.arange(GRID)
    turns = u[:, None] * u[None, :] % GRID
    angles = np.minimum(turns, GRID - turns) * (2.0 * math.pi / GRID)
    sign = np.where(turns <= GRID // 2, 1.0, -1.0)
    cosine = np.cos(angles).astype(ml_dtypes.bfloat16).astype(np.float64)
    sine = (sign * np.sin(angles)).astype(ml_dtypes.bfloat16).astype(np.float64)
    f = (u + GRID // 2) % GRID - GRID // 2
    phases = (f * f % (2 * GRID)) * (math.pi / GRID)
    chirp = np.cos(phases) - 1j * np.sin(phases)
    h = ((cosine - 1j * sine) * chirp) @ (cosine + 1j * sine) / GRID
    return np.stack([h.real, h.imag]).astype(ml_dtypes.bfloat16)


def cos_sin(phase):
    x = phase * 0.5
    z = x * x
    s = [(-1.0) ** i / math.factorial(2 * i + 1) for i in range(7)]
    c = [(-1.0) ** i / math.factorial(2 * i) for i in range(7)]
    ps = jnp.full_like(z, s[-1])
    for v in s[-2::-1]:
        ps = ps * z + v
    pc = jnp.full_like(z, c[-1])
    for v in c[-2::-1]:
        pc = pc * z + v
    sn = ps * x
    return 1.0 - 2.0 * sn * sn, 2.0 * sn * pc


def fold(v):
    tiles = [
        v[r : r + 8, c : c + 128] for r in range(0, v.shape[0], 8) for c in range(0, v.shape[1], 128)
    ]
    while len(tiles) > 1:
        tiles = [sum(tiles[i : i + 2]) for i in range(0, len(tiles), 2)]
    return tiles[0]


def kernel(
    f_in, b1_in, b2_in, p1_in, p2_in, h_in, m1_out, m2_out, a_out,
    f, b, ph, h, raws, px, prod, raw, irecv, wrecv, part, zrecv, precv, prow,
    both, full, m1, m1recv, mask, g, yb, s, arr, ls, ss, rs,
):
    mode = lax.axis_index("mode")
    row = lax.axis_index("row")
    zl, yc = mode // 8, lax.rem(mode, 8)
    zh, x = row // 4, lax.rem(row, 4)

    def row_peer(k):
        return (mode, lax.rem(row + k, 8))

    def x_peer(k):
        return (mode, zh * 4 + lax.rem(x + k, 4))

    def yc_peer(k):
        return (zl * 8 + lax.rem(yc + k, 8), row)

    def z_peer(k):
        return (lax.rem(zl + k, 8) * 8 + yc, row)

    def z16_peer(k):
        z = lax.rem(zh * 8 + zl + k, 16)
        return (lax.rem(z, 8) * 8 + yc, (z // 8) * 4 + x)

    def y_peer(k):
        return (zl * 8 + lax.rem(yc + 2 * k, 8), row)

    def c_peer(k):
        return (mode + 1 - 2 * lax.rem(mode, 2), row)

    def xyc_peer(k):
        at = lax.rem(x * 8 + yc + k, 32)
        return (zl * 8 + lax.rem(at, 8), zh * 4 + at // 8)

    bar = pltpu.get_barrier_semaphore()

    def greet(last, peer):
        def body(k, _):
            pl.semaphore_signal(bar, inc=1, device_id=peer(k), device_id_type=MESH)
            return 0

        lax.fori_loop(1, last, body, 0)

    greet(8, row_peer)
    greet(16, z16_peer)
    greet(32, xyc_peer)

    loads = [
        pltpu.make_async_copy(src, dst, ls.at[i])
        for i, (src, dst) in enumerate(
            [(f_in, f), (b1_in, b.at[0]), (p1_in, ph.at[0]), (h_in, h), (b2_in, b.at[1]), (p2_in, ph.at[1])]
        )
    ]
    for c in loads:
        c.start()

    used = [0, 0]
    sent = []

    class Stage:
        def __init__(self, src, dst, peer, all_sent, all_came=None, came=1):
            self.src, self.dst, self.peer, self.all_came = src, dst, peer, all_came
            self.s, self.r = used
            used[0] += 1
            used[1] += came
            sent.append(lambda: self.desc(0, 0, all_sent).wait_send())

        def desc(self, k, slot=0, whole=None):
            return pltpu.make_async_remote_copy(
                src_ref=self.src(k) if whole is None else whole,
                dst_ref=self.dst(k) if whole is None else whole,
                send_sem=ss.at[self.s], recv_sem=rs.at[self.r + slot],
                device_id=self.peer(1), device_id_type=MESH,
            )

        def start(self, k, slot=0):
            pltpu.make_async_remote_copy(
                src_ref=self.src(k), dst_ref=self.dst(k), send_sem=ss.at[self.s],
                recv_sem=rs.at[self.r + slot], device_id=self.peer(k), device_id_type=MESH,
            ).start()

        def start_all(self, last, first=1):
            def body(k, _):
                self.start(k)
                return 0

            lax.fori_loop(first, last, body, 0)

        def wait(self, whole=None, slot=0):
            self.desc(0, slot, self.all_came if whole is None else whole).wait_recv()

    def sixteen(j):
        return pl.ds(pl.multiple_of(j * 16, 16), 16)

    def products(i, front, put):
        back, phase = b.at[i], ph.at[i]

        def body(j, acc):
            rows = sixteen(j)
            fr, fi = front[0, rows, :].astype(F32), front[1, rows, :].astype(F32)
            br, bi = back[0, rows, :].astype(F32), back[1, rows, :].astype(F32)
            pr = br * fr + bi * fi
            pi = br * fi - bi * fr
            for q in range(8):
                cols = slice(q * 128, q * 128 + 128)
                put(j, q, jnp.stack([pr[:, cols], pi[:, cols]]).astype(BF16))
            c, sn = cos_sin(phase[rows, :])
            return acc[0] + fold(pr * c - pi * sn), acc[1] + fold(pr * sn + pi * c)

        zero = jnp.zeros((8, 128), F32)
        ir, ii = lax.fori_loop(0, 8, body, (zero, zero))
        irecv[i, 0, 0] = jnp.sum(ir, axis=0, keepdims=True)
        irecv[i, 0, 1] = jnp.sum(ii, axis=0, keepdims=True)

    def overlap(i):
        st = Stage(
            lambda k: irecv.at[i, 0], lambda k: irecv.at[i, k], row_peer,
            irecv.at[i, pl.ds(1, 7)], irecv.at[i, pl.ds(1, 7)],
        )
        st.start_all(8)
        return st

    def share_products(i):
        st = Stage(
            lambda k: prod.at[i, lax.rem(yc + k, 8)], lambda k: raw.at[i, k], yc_peer,
            raw.at[i, pl.ds(1, 7)], raw.at[i, pl.ds(1, 7)],
        )
        st.start_all(8)
        return st

    def share_weights(i):
        for q in range(2):
            wrecv[i, 0, q] = sum(irecv[i, k, q] for k in range(8))
        st = Stage(
            lambda k: wrecv.at[i, 0], lambda k: wrecv.at[i, k], yc_peer,
            wrecv.at[i, pl.ds(1, 7)], wrecv.at[i, pl.ds(1, 7)],
        )
        st.start_all(8)
        return st

    def reduced(i):
        weights = [
            [jnp.sum(wrecv[i, k, q], axis=1, keepdims=True) * (1.0 / GRID) for q in range(2)]
            for k in range(8)
        ]
        st = Stage(
            lambda k: part.at[i, k], lambda k: zrecv.at[i, k], z_peer,
            zrecv.at[i, pl.ds(1, 7)], zrecv.at[i, pl.ds(1, 7)],
        )

        def body(k, _):
            q = lax.rem(zl + k, 8)
            tr = jnp.zeros((16, 128), F32)
            ti = jnp.zeros((16, 128), F32)
            for m in range(8):
                pr, pi = raw[i, m, q, 0].astype(F32), raw[i, m, q, 1].astype(F32)
                wr, wi = weights[m]
                tr = tr + (wr * pr + wi * pi)
                ti = ti + (wr * pi - wi * pr)
            part[i, k, 0] = tr.astype(BF16)
            part[i, k, 1] = ti.astype(BF16)

            @pl.when(k < 8)
            def _():
                st.start(k)

            return 0

        lax.fori_loop(1, 9, body, 0)
        zrecv[i, 0] = part[i, 8]
        st.wait()
        return sum(zrecv[i, k].astype(F32) for k in range(8)).astype(BF16)

    def power_z(i, piece):
        v = piece.astype(F32)
        precv[i, 0] = jnp.sum(fold(v[0] * v[0] + v[1] * v[1]), axis=0, keepdims=True)
        st = Stage(
            lambda k: precv.at[i, 0], lambda k: precv.at[i, k], z16_peer,
            precv.at[i, pl.ds(1, 15)], precv.at[i, pl.ds(1, 15)],
        )
        st.start_all(16)
        return st

    def power_xy(i):
        prow[i, 0] = sum(precv[i, k] for k in range(16))
        st = Stage(
            lambda k: prow.at[i, 0], lambda k: prow.at[i, k], xyc_peer,
            prow.at[i, pl.ds(1, 31)], prow.at[i, pl.ds(1, 31)],
        )
        st.start_all(32)
        return st

    def power_floor(i):
        total = sum(prow[i, k] for k in range(32))
        mean = jnp.sum(total, axis=1, keepdims=True) * (1.0 / (GRID * GRID))
        return 0.25 * mean + 1e-6

    def masked(piece, floor):
        v = piece.astype(F32)
        scale = lax.rsqrt(v[0] * v[0] + v[1] * v[1] + floor)
        return (v[0] * scale).astype(BF16), (-v[1] * scale).astype(BF16)

    for c in loads[:3]:
        c.wait()

    def put_first(j, q, pair):
        px[q // 2, j // 4, lax.rem(j, 4) * 2 + q % 2] = pair

    products(0, f, put_first)
    pl.semaphore_wait(bar, 7 + 15 + 31)
    over = overlap(0)
    turn = Stage(
        lambda k: px.at[lax.rem(x + k, 4)], lambda k: prod.at[0, pl.ds(2 * x, 2)], x_peer,
        prod.at[0, pl.ds(0, 6)], prod.at[0, pl.ds(0, 6)],
    )
    turn.start_all(4)

    def block(r, half):
        return pl.ds(pl.multiple_of(lax.rem(r, 4) * 256 + half * 128, 128), 128)

    moves = []
    for half in range(2):
        st = Stage(
            lambda k, half=half: f.at[:, :, block(row + k, half)],
            lambda k, half=half: raws.at[half, row], row_peer,
            raws.at[half, pl.ds(0, 7)], raws.at[half, pl.ds(0, 7)],
        )
        moves.append(st)

    def far(k):
        return (lax.rem(row + k, 8) // 4) != zh

    def move(half, want_far):
        def body(k, _):
            @pl.when(far(k) if want_far else jnp.logical_not(far(k)))
            def _():
                moves[half].start(k)

            return 0

        lax.fori_loop(1, 8, body, 0)

    move(0, True)
    move(1, True)
    own = [
        pltpu.make_async_copy(f.at[:, :, block(row, half)], raws.at[half, row], ls.at[9 + half])
        for half in range(2)
    ]
    for c in own:
        c.start()
    prod[0, pl.ds(2 * x, 2)] = px[x]
    turn.wait()
    share = share_products(0)
    move(0, False)
    move(1, False)
    over.wait()
    weight = share_weights(0)
    raw[0, 0] = prod[0, yc]
    share.wait()
    weight.wait()
    piece = reduced(0)
    both[yc, 2 * zl + zh] = piece
    gather_z = Stage(
        lambda k: both.at[yc, 2 * zl + zh], lambda k: both.at[yc, 2 * zl + zh], z16_peer,
        both.at[yc, pl.ds(0, 15)], both.at[yc, pl.ds(0, 15)],
    )
    gather_z.start_all(16)
    pz = power_z(0, piece)
    gather_z.wait()
    gather_y = Stage(
        lambda k: both.at[yc], lambda k: both.at[yc], y_peer, both.at[pl.ds(0, 3)], None, 3
    )
    for o in range(1, 4):
        gather_y.start(o, o - 1)
    gather_c = Stage(
        lambda k: both.at[lax.rem(yc + 2 * k, 8)], lambda k: both.at[lax.rem(yc + 2 * k, 8)], c_peer,
        both.at[pl.ds(0, 4)], both.at[pl.ds(0, 4)],
    )
    gather_c.start(4)
    pz.wait()
    pxy = power_xy(0)
    for o in range(1, 4):
        gather_y.wait(both.at[0], o - 1)
        gather_c.start(4 - o)
    pxy.wait()
    floor = power_floor(0)
    gather_c.wait()
    for c in own:
        c.wait()
    for c in loads[3:]:
        c.wait()

    to_rows = []
    for half in range(2):
        moves[half].wait()

        def apply(j, _, half=half):
            z, n = j // 8, lax.rem(j, 8)
            for u in range(4):
                mr, mi = masked(both[n, (2 * u + half) * 2 + z], floor)
                at = lax.rem(n, 2) * 64 + u * 16

                @pl.when(z == zh)
                def _():
                    m1[n, 2 * u + half, 0] = mr
                    m1[n, 2 * u + half, 1] = mi

                rows = pl.ds(pl.multiple_of(at, 16), 16)
                fr = raws[half, z * 4 + n // 2, 0, rows, :].astype(F32)
                fi = raws[half, z * 4 + n // 2, 1, rows, :].astype(F32)
                mr, mi = mr.astype(F32), mi.astype(F32)
                rows = pl.ds(pl.multiple_of(j * 64 + u * 16, 16), 16)
                g[half, rows, 0:128] = (fr * mr - fi * mi).astype(BF16)
                g[half, rows, 128:256] = (fr * mi + fi * mr).astype(BF16)
            return 0

        lax.fori_loop(0, 16, apply, 0)
        st = Stage(
            lambda k, half=half: yb.at[half, lax.rem(x + k, 4)],
            lambda k, half=half: s.at[:, :, pl.ds(pl.multiple_of(x * 256 + half * 128, 128), 128)],
            x_peer, yb.at[half, pl.ds(0, 3)], yb.at[half, pl.ds(0, 3)],
        )
        to_rows.append(st)
        for n in range(2):
            rows = pl.ds(pl.multiple_of(zh * 512 + n * 256, 256), 256)
            a = jnp.dot(h[0, rows, :], g[half], preferred_element_type=F32)
            c = jnp.dot(h[1, rows, :], g[half], preferred_element_type=F32)
            yr = (a[:, :128] - c[:, 128:]).astype(BF16)
            yi = (a[:, 128:] + c[:, :128]).astype(BF16)
            for e in range(2):
                to = 2 * n + e
                yb[half, to, 0] = yr[e * ROWS : e * ROWS + ROWS]
                yb[half, to, 1] = yi[e * ROWS : e * ROWS + ROWS]

                @pl.when(to != x)
                def _(to=to, st=st):
                    st.start(lax.rem(to - x + 4, 4))

        s[:, :, pl.ds(pl.multiple_of(x * 256 + half * 128, 128), 128)] = yb[half, x]

    for half in range(2):
        to_rows[half].wait()

    def columns(n, _):
        cols = pl.ds(pl.multiple_of(n * 256, 256), 256)
        field = s[...].reshape(2 * ROWS, GRID)
        a = jnp.dot(field, h[0, :, cols], preferred_element_type=F32)
        c = jnp.dot(field, h[1, :, cols], preferred_element_type=F32)
        arr[0, :, cols] = (a[:ROWS] - c[ROWS:]).astype(BF16)
        arr[1, :, cols] = (c[:ROWS] + a[ROWS:]).astype(BF16)
        return 0

    lax.fori_loop(0, 4, columns, 0)
    outs = [pltpu.make_async_copy(arr, a_out, ls.at[6])]
    outs[0].start()

    def put_second(j, q, pair):
        prod[1, j, q] = pair

    products(1, arr, put_second)
    over = overlap(1)
    share = share_products(1)
    back1 = Stage(
        lambda k: m1.at[pl.ds(2 * lax.rem(x + k, 4), 2)], lambda k: m1recv.at[x], x_peer,
        m1recv.at[pl.ds(0, 3)], m1recv.at[pl.ds(0, 3)],
    )
    back1.start_all(4)
    m1recv[x] = m1[pl.ds(2 * x, 2)]
    over.wait()
    weight = share_weights(1)
    raw[1, 0] = prod[1, yc]
    share.wait()
    weight.wait()
    piece = reduced(1)
    full[yc, zl] = piece
    gather_z = Stage(
        lambda k: full.at[yc, zl], lambda k: full.at[yc, zl], z_peer, full.at[yc, pl.ds(0, 7)], None, 8
    )

    def spread(k, _):
        gather_z.start(k, zl)
        return 0

    lax.fori_loop(1, 8, spread, 0)
    pz = power_z(1, piece)

    gather_y2 = [
        Stage(lambda q: full.at[yc, q], lambda q: full.at[yc, q], lambda k, o=o: y_peer(o), full.at[yc], full.at[0])
        for o in range(1, 4)
    ]

    def onward(q):
        for st in gather_y2:
            st.start(q)

    onward(zl)

    def forward(d, _):
        for q in (zl - d, zl + d):

            @pl.when((q >= 0) & (q < 8))
            def _():
                gather_z.wait(full.at[yc, q], q)
                onward(q)

        return 0

    lax.fori_loop(1, 8, forward, 0)
    gather_c = Stage(
        lambda k: full.at[lax.rem(yc + 2 * k, 8)], lambda k: full.at[lax.rem(yc + 2 * k, 8)], c_peer,
        full.at[pl.ds(0, 4)], full.at[pl.ds(0, 4)],
    )
    gather_c.start(4)
    pz.wait()
    pxy = power_xy(1)
    for o in range(1, 4):
        gather_y2[o - 1].wait()
        gather_c.start(4 - o)

    back1.wait()

    def lay(j, _):
        for q in range(8):
            v = m1recv[q // 2, j // 4, lax.rem(j, 4) * 2 + q % 2]
            mask[0, 0, sixteen(j), q * 128 : q * 128 + 128] = v[0]
            mask[0, 1, sixteen(j), q * 128 : q * 128 + 128] = v[1]
        return 0

    lax.fori_loop(0, 8, lay, 0)
    outs.append(pltpu.make_async_copy(mask.at[0], m1_out, ls.at[7]))
    outs[1].start()
    pxy.wait()
    floor2 = power_floor(1)
    gather_c.wait()

    def finish(j, _):
        for q in range(8):
            mr, mi = masked(full[j, q], floor2)
            mask[1, 0, sixteen(j), q * 128 : q * 128 + 128] = mr
            mask[1, 1, sixteen(j), q * 128 : q * 128 + 128] = mi
        return 0

    lax.fori_loop(0, 8, finish, 0)
    outs.append(pltpu.make_async_copy(mask.at[1], m2_out, ls.at[8]))
    outs[2].start()
    for w in sent:
        w()
    for c in outs:
        c.wait()


def on_device(forward, backward_first, backward_second, phase_first, phase_second):
    hbm = pl.BlockSpec(memory_space=pl.ANY)
    block = (2, ROWS, GRID)
    tile = (2, 16, 128)
    m1, m2, arrived = pl.pallas_call(
        kernel,
        out_shape=[jax.ShapeDtypeStruct(block, BF16)] * 3,
        in_specs=[hbm] * 6,
        out_specs=[hbm] * 3,
        scratch_shapes=[
            pltpu.VMEM(block, BF16),
            pltpu.VMEM((2, *block), BF16),
            pltpu.VMEM((2, ROWS, GRID), F32),
            pltpu.VMEM((2, GRID, GRID), BF16),
            pltpu.VMEM((2, 8, 2, ROWS, 128), BF16),
            pltpu.VMEM((4, 2, 8, *tile), BF16),
            pltpu.VMEM((2, 8, 8, *tile), BF16),
            pltpu.VMEM((2, 8, 8, *tile), BF16),
            pltpu.VMEM((2, 8, 2, 1, 128), F32),
            pltpu.VMEM((2, 8, 2, 1, 128), F32),
            pltpu.VMEM((2, 9, *tile), BF16),
            pltpu.VMEM((2, 8, *tile), BF16),
            pltpu.VMEM((2, 16, 1, 128), F32),
            pltpu.VMEM((2, 32, 1, 128), F32),
            pltpu.VMEM((8, 16, *tile), BF16),
            pltpu.VMEM((8, 8, *tile), BF16),
            pltpu.VMEM((8, 8, *tile), BF16),
            pltpu.VMEM((4, 2, 8, *tile), BF16),
            pltpu.VMEM((2, *block), BF16),
            pltpu.VMEM((2, GRID, 256), BF16),
            pltpu.VMEM((2, 4, 2, ROWS, 128), BF16),
            pltpu.VMEM(block, BF16),
            pltpu.VMEM(block, BF16),
            pltpu.SemaphoreType.DMA((11,)),
            pltpu.SemaphoreType.DMA((32,)),
            pltpu.SemaphoreType.DMA((40,)),
        ],
        compiler_params=pltpu.CompilerParams(
            collective_id=0, has_side_effects=True, vmem_limit_bytes=60 * 2**20
        ),
    )(
        forward[0], backward_first[0], backward_second[0], phase_first, phase_second,
        jnp.asarray(propagator()),
    )
    return m1, m2, arrived[None]


def solution(mesh):
    in_specs = (
        P("mode", None, "row", None),
        P("mode", None, "row", None),
        P("mode", None, "row", None),
        P("row", None),
        P("row", None),
    )
    out_specs = (P(None, "row", None), P(None, "row", None), P("mode", None, "row", None))
    return jax.shard_map(
        on_device, mesh=mesh, in_specs=in_specs, out_specs=out_specs, check_vma=False
    )
```

time: 159 us -> 139 us (0.87)
  Pallas kernels: 152 us -> 133 us
    pallas_call x1, Pallas kernels: 152 us -> 133 us  [on_device(): pl.pallas_call(kernel, out_shape=[jax.ShapeDtypeStruct(block, BF16)] * 3,...]
where the time goes in v3:
time: 139 us
  Pallas kernels  133 us (96%)
  local copies, waits for them, and re-layouts  5.6 us (4%)
    pallas_call x1, Pallas kernels, on_device(): pl.pallas_call(kernel, out_shape=[jax.ShapeDtypeStruct(block, BF16)] * 3,...  133 us
    unnamed x3, local copies, waits for them, and re-layouts  5.6 us

profile of v3, /device:TPU:1, one launch (start us, length us, event | category | flops | bytes accessed | tf_op | source)
XLA Modules:
  0.0 139.2 jit_solution(1309043280736158094)
XLA Ops:
  0.6 132.9 %shard_map.85 = (bf16[2,128,1024]{2,1,0:T(8,128)(2,1)}, bf16[2,128,1024]{2,1,0:T(8,128)(2,1)}, bf16[2,128,1024]{2,1,0:T(8,128)(2,1)}) custom-call(bf16[2,128,1024]{2,1,0:T(8,128)(2,1)} %bitcast.5, bf16[2,128,1024]{2,1,0:T(8,128)(2,1)} %bitcast.6, bf16[2,128,1024]{2,1,0:T(8,128)(2,1)} %bitcast.7, f32[128,1024]{1,0:T(8,128)} %p1_in.1, f32[128,1024]{1,0:T(8,128)} %p2_in.1, ...), custom_call_target="tpu_custom_call" | custom-call | tf_op jit(solution)/shard_map/pallas_call | solution.py:516
  133.6 1.9 %copy.12 = bf16[2,128,1024]{2,1,0:T(8,128)(2,1)} copy(bf16[2,128,1024]{2,1,0:T(8,128)(2,1)} %get-tuple-element.12) | data formatting | bytes 1048576
  135.4 1.9 %copy.13 = bf16[2,128,1024]{2,1,0:T(8,128)(2,1)} copy(bf16[2,128,1024]{2,1,0:T(8,128)(2,1)} %get-tuple-element.13) | data formatting | bytes 1048576
  137.3 1.9 %copy.14 = bf16[1,2,128,1024]{3,2,1,0:T(8,128)(2,1)} copy(bf16[1,2,128,1024]{3,2,1,0:T(8,128)(2,1)} %bitcast.4) | data formatting | bytes 1048576

commit v4 on v3

--- a/solution.py
+++ b/solution.py
@@ -58,7 +58,7 @@
 
 def kernel(
     f_in, b1_in, b2_in, p1_in, p2_in, h_in, m1_out, m2_out, a_out,
-    f, b, ph, h, raws, px, prod, raw, irecv, wrecv, part, zrecv, precv, prow,
+    f, b, ph, cs, h, raws, px, prod, raw, irecv, wrecv, part, zrecv, precv, prow,
     both, full, m1, m1recv, mask, g, yb, s, arr, ls, ss, rs,
 ):
     mode = lax.axis_index("mode")
@@ -123,7 +123,8 @@
             self.s, self.r = used
             used[0] += 1
             used[1] += came
-            sent.append(lambda: self.desc(0, 0, all_sent).wait_send())
+            self.left = lambda: self.desc(0, 0, all_sent).wait_send()
+            sent.append(self)
 
         def desc(self, k, slot=0, whole=None):
             return pltpu.make_async_remote_copy(
@@ -152,8 +153,8 @@
     def sixteen(j):
         return pl.ds(pl.multiple_of(j * 16, 16), 16)
 
-    def products(i, front, put):
-        back, phase = b.at[i], ph.at[i]
+    def products(i, front, put, turned):
+        back = b.at[i]
 
         def body(j, acc):
             rows = sixteen(j)
@@ -164,7 +165,7 @@
             for q in range(8):
                 cols = slice(q * 128, q * 128 + 128)
                 put(j, q, jnp.stack([pr[:, cols], pi[:, cols]]).astype(BF16))
-            c, sn = cos_sin(phase[rows, :])
+            c, sn = turned(rows)
             return acc[0] + fold(pr * c - pi * sn), acc[1] + fold(pr * sn + pi * c)
 
         zero = jnp.zeros((8, 128), F32)
@@ -266,7 +267,7 @@
     def put_first(j, q, pair):
         px[q // 2, j // 4, lax.rem(j, 4) * 2 + q % 2] = pair
 
-    products(0, f, put_first)
+    products(0, f, put_first, lambda rows: cos_sin(ph[0, rows, :]))
     pl.semaphore_wait(bar, 7 + 15 + 31)
     over = overlap(0)
     turn = Stage(
@@ -279,29 +280,30 @@
         return pl.ds(pl.multiple_of(lax.rem(r, 4) * 256 + half * 128, 128), 128)
 
     moves = []
-    for half in range(2):
-        st = Stage(
-            lambda k, half=half: f.at[:, :, block(row + k, half)],
-            lambda k, half=half: raws.at[half, row], row_peer,
-            raws.at[half, pl.ds(0, 7)], raws.at[half, pl.ds(0, 7)],
+    parts = ((0, 0, 128), (1, 0, 64), (1, 64, 64))
+    for half, top, size in parts:
+        some = pl.ds(top, size)
+        st = Stage(
+            lambda k, half=half, some=some: f.at[:, some, block(row + k, half)],
+            lambda k, half=half, some=some: raws.at[half, row, :, some, :], row_peer,
+            raws.at[half, pl.ds(0, 7), :, some, :], raws.at[half, pl.ds(0, 7), :, some, :],
         )
         moves.append(st)
 
     def far(k):
         return (lax.rem(row + k, 8) // 4) != zh
 
-    def move(half, want_far):
+    def move(part, want_far):
         def body(k, _):
             @pl.when(far(k) if want_far else jnp.logical_not(far(k)))
             def _():
-                moves[half].start(k)
+                moves[part].start(k)
 
             return 0
 
         lax.fori_loop(1, 8, body, 0)
 
     move(0, True)
-    move(1, True)
     own = [
         pltpu.make_async_copy(f.at[:, :, block(row, half)], raws.at[half, row], ls.at[9 + half])
         for half in range(2)
@@ -311,8 +313,8 @@
     prod[0, pl.ds(2 * x, 2)] = px[x]
     turn.wait()
     share = share_products(0)
-    move(0, False)
-    move(1, False)
+    for p in range(3):
+        move(p, False)
     over.wait()
     weight = share_weights(0)
     raw[0, 0] = prod[0, yc]
@@ -327,6 +329,8 @@
     gather_z.start_all(16)
     pz = power_z(0, piece)
     gather_z.wait()
+    move(1, True)
+    move(2, True)
     gather_y = Stage(
         lambda k: both.at[yc], lambda k: both.at[yc], y_peer, both.at[pl.ds(0, 3)], None, 3
     )
@@ -345,30 +349,53 @@
     pxy.wait()
     floor = power_floor(0)
     gather_c.wait()
+
+    def make_mask(n, _):
+        for q in range(8):
+            for z in range(2):
+                mr, mi = masked(both[n, 2 * q + z], floor)
+                both[n, 2 * q + z, 0] = mr
+                both[n, 2 * q + z, 1] = mi
+            m1[n, q] = both[n, 2 * q + zh]
+        return 0
+
+    early = [gather_z, gather_y, gather_c]
+    for st in early:
+        st.left()
+    lax.fori_loop(0, 8, make_mask, 0)
+    back1 = Stage(
+        lambda k: m1.at[pl.ds(2 * lax.rem(x + k, 4), 2)], lambda k: m1recv.at[x], x_peer,
+        m1recv.at[pl.ds(0, 3)], m1recv.at[pl.ds(0, 3)],
+    )
+    back1.start_all(4)
+    m1recv[x] = m1[pl.ds(2 * x, 2)]
     for c in own:
         c.wait()
     for c in loads[3:]:
         c.wait()
 
+    def turn_phase(j, _):
+        c, sn = cos_sin(ph[1, sixteen(j), :])
+        cs[0, sixteen(j), :] = c
+        cs[1, sixteen(j), :] = sn
+        return 0
+
+    lax.fori_loop(0, 8, turn_phase, 0)
+
     to_rows = []
     for half in range(2):
-        moves[half].wait()
+        for p in (0,) if half == 0 else (1, 2):
+            moves[p].wait()
 
         def apply(j, _, half=half):
             z, n = j // 8, lax.rem(j, 8)
             for u in range(4):
-                mr, mi = masked(both[n, (2 * u + half) * 2 + z], floor)
+                v = both[n, (2 * u + half) * 2 + z].astype(F32)
                 at = lax.rem(n, 2) * 64 + u * 16
-
-                @pl.when(z == zh)
-                def _():
-                    m1[n, 2 * u + half, 0] = mr
-                    m1[n, 2 * u + half, 1] = mi
-
                 rows = pl.ds(pl.multiple_of(at, 16), 16)
                 fr = raws[half, z * 4 + n // 2, 0, rows, :].astype(F32)
                 fi = raws[half, z * 4 + n // 2, 1, rows, :].astype(F32)
-                mr, mi = mr.astype(F32), mi.astype(F32)
+                mr, mi = v[0], v[1]
                 rows = pl.ds(pl.multiple_of(j * 64 + u * 16, 16), 16)
                 g[half, rows, 0:128] = (fr * mr - fi * mi).astype(BF16)
                 g[half, rows, 128:256] = (fr * mi + fi * mr).astype(BF16)
@@ -417,15 +444,9 @@
     def put_second(j, q, pair):
         prod[1, j, q] = pair
 
-    products(1, arr, put_second)
+    products(1, arr, put_second, lambda rows: (cs[0, rows, :], cs[1, rows, :]))
     over = overlap(1)
     share = share_products(1)
-    back1 = Stage(
-        lambda k: m1.at[pl.ds(2 * lax.rem(x + k, 4), 2)], lambda k: m1recv.at[x], x_peer,
-        m1recv.at[pl.ds(0, 3)], m1recv.at[pl.ds(0, 3)],
-    )
-    back1.start_all(4)
-    m1recv[x] = m1[pl.ds(2 * x, 2)]
     over.wait()
     weight = share_weights(1)
     raw[1, 0] = prod[1, yc]
@@ -503,8 +524,9 @@
     lax.fori_loop(0, 8, finish, 0)
     outs.append(pltpu.make_async_copy(mask.at[1], m2_out, ls.at[8]))
     outs[2].start()
-    for w in sent:
-        w()
+    for st in sent:
+        if st not in early:
+            st.left()
     for c in outs:
         c.wait()
 
@@ -521,6 +543,7 @@
         scratch_shapes=[
             pltpu.VMEM(block, BF16),
             pltpu.VMEM((2, *block), BF16),
+            pltpu.VMEM((2, ROWS, GRID), F32),
             pltpu.VMEM((2, ROWS, GRID), F32),
             pltpu.VMEM((2, GRID, GRID), BF16),
             pltpu.VMEM((2, 8, 2, ROWS, 128), BF16),
@@ -547,7 +570,7 @@
             pltpu.SemaphoreType.DMA((40,)),
         ],
         compiler_params=pltpu.CompilerParams(
-            collective_id=0, has_side_effects=True, vmem_limit_bytes=60 * 2**20
+            collective_id=0, has_side_effects=True, vmem_limit_bytes=52 * 2**20
         ),
     )(
         forward[0], backward_first[0], backward_second[0], phase_first, phase_second,

time: 139 us -> 130 us (0.935)
  Pallas kernels: 133 us -> 127 us
  local copies, waits for them, and re-layouts: 5.6 us -> 2.38 us
    pallas_call x1, Pallas kernels: 133 us -> 127 us  [on_device(): pl.pallas_call(kernel, out_shape=[jax.ShapeDtypeStruct(block, BF16)] * 3,...]
    unnamed x3, local copies, waits for them, and re-layouts: 5.6 us -> 2.38 us
where the time goes in v4:
time: 130 us
  Pallas kernels  127 us (98%)
  local copies, waits for them, and re-layouts  2.38 us (2%)
    pallas_call x1, Pallas kernels, on_device(): pl.pallas_call(kernel, out_shape=[jax.ShapeDtypeStruct(block, BF16)] * 3,...  127 us

profile of v4, /device:TPU:1, one launch (start us, length us, event | category | flops | bytes accessed | tf_op | source)
XLA Modules:
  0.0 129.6 jit_solution(17075098331764143615)
XLA Ops:
  0.6 126.6 %shard_map.85 = (bf16[2,128,1024]{2,1,0:T(8,128)(2,1)S(1)}, bf16[2,128,1024]{2,1,0:T(8,128)(2,1)S(1)}, bf16[2,128,1024]{2,1,0:T(8,128)(2,1)S(1)}) custom-call(bf16[2,128,1024]{2,1,0:T(8,128)(2,1)} %bitcast.5, bf16[2,128,1024]{2,1,0:T(8,128)(2,1)} %bitcast.6, bf16[2,128,1024]{2,1,0:T(8,128)(2,1)} %bitcast.7, f32[128,1024]{1,0:T(8,128)} %p1_in.1, ...), custom_call_target="tpu_custom_call" | custom-call | tf_op jit(solution)/shard_map/pallas_call | solution.py:538
  127.2 0.8 copy.12
  128.0 0.8 copy.13
  128.8 0.8 copy.14

commit v5 on v4

--- a/solution.py
+++ b/solution.py
@@ -58,7 +58,7 @@
 
 def kernel(
     f_in, b1_in, b2_in, p1_in, p2_in, h_in, m1_out, m2_out, a_out,
-    f, b, ph, cs, h, raws, px, prod, raw, irecv, wrecv, part, zrecv, precv, prow,
+    f, b, ph, cs, h, hk, acc, raws, px, prod, raw, irecv, wrecv, part, zrecv, precv, prow,
     both, full, m1, m1recv, mask, g, yb, s, arr, ls, ss, rs,
 ):
     mode = lax.axis_index("mode")
@@ -110,6 +110,14 @@
         for i, (src, dst) in enumerate(
             [(f_in, f), (b1_in, b.at[0]), (p1_in, ph.at[0]), (h_in, h), (b2_in, b.at[1]), (p2_in, ph.at[1])]
         )
+    ]
+    loads += [
+        pltpu.make_async_copy(
+            h_in.at[:, pl.ds(v * 256 + half * 128, 128), :],
+            hk.at[:, half, pl.ds(v * 128, 128), :], ls.at[11 + half * 4 + v],
+        )
+        for half in range(2)
+        for v in range(4)
     ]
     for c in loads:
         c.start()
@@ -382,7 +390,20 @@
 
     lax.fori_loop(0, 8, turn_phase, 0)
 
-    to_rows = []
+    def columns(half, n, _):
+        cols = pl.ds(pl.multiple_of(n * 256, 256), 256)
+        field = s[half].reshape(2 * ROWS, GRID // 2)
+        a = jnp.dot(field, hk[0, half, :, cols], preferred_element_type=F32)
+        c = jnp.dot(field, hk[1, half, :, cols], preferred_element_type=F32)
+        re, im = a[:ROWS] - c[ROWS:], c[:ROWS] + a[ROWS:]
+        if half == 0:
+            acc[0, :, cols] = re
+            acc[1, :, cols] = im
+        else:
+            arr[0, :, cols] = (acc[0, :, cols] + re).astype(BF16)
+            arr[1, :, cols] = (acc[1, :, cols] + im).astype(BF16)
+        return 0
+
     for half in range(2):
         for p in (0,) if half == 0 else (1, 2):
             moves[p].wait()
@@ -404,10 +425,9 @@
         lax.fori_loop(0, 16, apply, 0)
         st = Stage(
             lambda k, half=half: yb.at[half, lax.rem(x + k, 4)],
-            lambda k, half=half: s.at[:, :, pl.ds(pl.multiple_of(x * 256 + half * 128, 128), 128)],
+            lambda k, half=half: s.at[half, :, :, pl.ds(pl.multiple_of(x * 128, 128), 128)],
             x_peer, yb.at[half, pl.ds(0, 3)], yb.at[half, pl.ds(0, 3)],
         )
-        to_rows.append(st)
         for n in range(2):
             rows = pl.ds(pl.multiple_of(zh * 512 + n * 256, 256), 256)
             a = jnp.dot(h[0, rows, :], g[half], preferred_element_type=F32)
@@ -423,21 +443,10 @@
                 def _(to=to, st=st):
                     st.start(lax.rem(to - x + 4, 4))
 
-        s[:, :, pl.ds(pl.multiple_of(x * 256 + half * 128, 128), 128)] = yb[half, x]
-
-    for half in range(2):
-        to_rows[half].wait()
-
-    def columns(n, _):
-        cols = pl.ds(pl.multiple_of(n * 256, 256), 256)
-        field = s[...].reshape(2 * ROWS, GRID)
-        a = jnp.dot(field, h[0, :, cols], preferred_element_type=F32)
-        c = jnp.dot(field, h[1, :, cols], preferred_element_type=F32)
-        arr[0, :, cols] = (a[:ROWS] - c[ROWS:]).astype(BF16)
-        arr[1, :, cols] = (c[:ROWS] + a[ROWS:]).astype(BF16)
-        return 0
-
-    lax.fori_loop(0, 4, columns, 0)
+        s[half, :, :, pl.ds(pl.multiple_of(x * 128, 128), 128)] = yb[half, x]
+        st.wait()
+        lax.fori_loop(0, 4, functools.partial(columns, half), 0)
+
     outs = [pltpu.make_async_copy(arr, a_out, ls.at[6])]
     outs[0].start()
 
@@ -462,8 +471,8 @@
         gather_z.start(k, zl)
         return 0
 
+    pz = power_z(1, piece)
     lax.fori_loop(1, 8, spread, 0)
-    pz = power_z(1, piece)
 
     gather_y2 = [
         Stage(lambda q: full.at[yc, q], lambda q: full.at[yc, q], lambda k, o=o: y_peer(o), full.at[yc], full.at[0])
@@ -528,6 +537,20 @@
         if st not in early:
             st.left()
     for c in outs:
+        c.wait()
+
+
+def write_out(*refs):
+    sems = refs[6]
+    copies = []
+    for src, dst in zip(refs[:3], refs[3:6]):
+        for i in range(4):
+            rows = pl.ds(i * 32, 32)
+            copies.append(
+                pltpu.make_async_copy(src.at[:, rows], dst.at[:, rows], sems.at[len(copies)])
+            )
+            copies[-1].start()
+    for c in copies:
         c.wait()
 
 
@@ -546,6 +569,8 @@
             pltpu.VMEM((2, ROWS, GRID), F32),
             pltpu.VMEM((2, ROWS, GRID), F32),
             pltpu.VMEM((2, GRID, GRID), BF16),
+            pltpu.VMEM((2, 2, GRID // 2, GRID), BF16),
+            pltpu.VMEM(block, F32),
             pltpu.VMEM((2, 8, 2, ROWS, 128), BF16),
             pltpu.VMEM((4, 2, 8, *tile), BF16),
             pltpu.VMEM((2, 8, 8, *tile), BF16),
@@ -563,9 +588,9 @@
             pltpu.VMEM((2, *block), BF16),
             pltpu.VMEM((2, GRID, 256), BF16),
             pltpu.VMEM((2, 4, 2, ROWS, 128), BF16),
+            pltpu.VMEM((2, 2, ROWS, GRID // 2), BF16),
             pltpu.VMEM(block, BF16),
-            pltpu.VMEM(block, BF16),
-            pltpu.SemaphoreType.DMA((11,)),
+            pltpu.SemaphoreType.DMA((19,)),
             pltpu.SemaphoreType.DMA((32,)),
             pltpu.SemaphoreType.DMA((40,)),
         ],
@@ -576,6 +601,14 @@
         forward[0], backward_first[0], backward_second[0], phase_first, phase_second,
         jnp.asarray(propagator()),
     )
+    m1, m2, arrived = pl.pallas_call(
+        write_out,
+        out_shape=[jax.ShapeDtypeStruct(block, BF16)] * 3,
+        in_specs=[hbm] * 3,
+        out_specs=[hbm] * 3,
+        scratch_shapes=[pltpu.SemaphoreType.DMA((12,))],
+        compiler_params=pltpu.CompilerParams(vmem_limit_bytes=2**20),
+    )(m1, m2, arrived)
     return m1, m2, arrived[None]
 
 

time: 130 us -> 128 us (0.985)
  local copies, waits for them, and re-layouts: 2.38 us -> 0 us
    unnamed x3 -> x0, local copies, waits for them, and re-layouts: 2.38 us -> none
where the time goes in v5:
time: 128 us; the launch traced here: 127 us
  Pallas kernels  127 us (99%)
    pallas_call x1, Pallas kernels, on_device(): pl.pallas_call(kernel, out_shape=[jax.ShapeDtypeStruct(block, BF16)] * 3,...  126 us

profile of v5, /device:TPU:1, one launch (start us, length us, event | category | flops | bytes accessed | tf_op | source)
XLA Modules:
  0.0 127.5 jit_solution(11514184510033534916)
XLA Ops:
  0.6 125.6 %shard_map.85 = (bf16[2,128,1024]{2,1,0:T(8,128)(2,1)S(1)}, bf16[2,128,1024]{2,1,0:T(8,128)(2,1)S(1)}, bf16[2,128,1024]{2,1,0:T(8,128)(2,1)S(1)}) custom-call(bf16[2,128,1024]{2,1,0:T(8,128)(2,1)} %bitcast.4, bf16[2,128,1024]{2,1,0:T(8,128)(2,1)} %bitcast.5, bf16[2,128,1024]{2,1,0:T(8,128)(2,1)} %bitcast.6, f32[128,1024]{1,0:T(8,128)} %p1_in.1, ...), custom_call_target="tpu_custom_call" | custom-call | tf_op jit(solution)/shard_map/pallas_call | solution.py:561
  126.2 1.2 shard_map.86

commit v6 on v5

--- a/solution.py
+++ b/solution.py
@@ -58,7 +58,7 @@
 
 def kernel(
     f_in, b1_in, b2_in, p1_in, p2_in, h_in, m1_out, m2_out, a_out,
-    f, b, ph, cs, h, hk, acc, raws, px, prod, raw, irecv, wrecv, part, zrecv, precv, prow,
+    f, b, ph, w, wh, whrecv, h, hk, acc, raws, px, prod, raw, irecv, wrecv, part, zrecv, precv, prow,
     both, full, m1, m1recv, mask, g, yb, s, arr, ls, ss, rs,
 ):
     mode = lax.axis_index("mode")
@@ -173,13 +173,16 @@
             for q in range(8):
                 cols = slice(q * 128, q * 128 + 128)
                 put(j, q, jnp.stack([pr[:, cols], pi[:, cols]]).astype(BF16))
+            if turned is None:
+                return acc
             c, sn = turned(rows)
             return acc[0] + fold(pr * c - pi * sn), acc[1] + fold(pr * sn + pi * c)
 
         zero = jnp.zeros((8, 128), F32)
         ir, ii = lax.fori_loop(0, 8, body, (zero, zero))
-        irecv[i, 0, 0] = jnp.sum(ir, axis=0, keepdims=True)
-        irecv[i, 0, 1] = jnp.sum(ii, axis=0, keepdims=True)
+        if turned is not None:
+            irecv[i, 0, 0] = jnp.sum(ir, axis=0, keepdims=True)
+            irecv[i, 0, 1] = jnp.sum(ii, axis=0, keepdims=True)
 
     def overlap(i):
         st = Stage(
@@ -383,12 +386,31 @@
         c.wait()
 
     def turn_phase(j, _):
-        c, sn = cos_sin(ph[1, sixteen(j), :])
-        cs[0, sixteen(j), :] = c
-        cs[1, sixteen(j), :] = sn
+        rows = sixteen(j)
+        c, sn = cos_sin(ph[1, rows, :])
+        br, bi = b[1, 0, rows, :].astype(F32), b[1, 1, rows, :].astype(F32)
+        w[0, rows, :] = (br * c + bi * sn).astype(BF16)
+        w[1, rows, :] = (br * sn - bi * c).astype(BF16)
         return 0
 
     lax.fori_loop(0, 8, turn_phase, 0)
+    turn_w = Stage(
+        lambda k: wh.at[lax.rem(x + k, 4)], lambda k: whrecv.at[x], x_peer,
+        whrecv.at[pl.ds(0, 3)], whrecv.at[pl.ds(0, 3)],
+    )
+
+    def adjoint(n, _):
+        cols = pl.ds(pl.multiple_of(n * 256, 256), 256)
+        field = w[...].reshape(2 * ROWS, GRID)
+        a = jnp.dot(field, h[0, :, cols], preferred_element_type=F32)
+        c = jnp.dot(field, h[1, :, cols], preferred_element_type=F32)
+        wh[n, 0] = (a[:ROWS] - c[ROWS:]).astype(BF16)
+        wh[n, 1] = (c[:ROWS] + a[ROWS:]).astype(BF16)
+        return 0
+
+    lax.fori_loop(0, 4, adjoint, 0)
+    turn_w.start_all(4)
+    whrecv[x] = wh[x]
 
     def columns(half, n, _):
         cols = pl.ds(pl.multiple_of(n * 256, 256), 256)
@@ -428,6 +450,9 @@
             lambda k, half=half: s.at[half, :, :, pl.ds(pl.multiple_of(x * 128, 128), 128)],
             x_peer, yb.at[half, pl.ds(0, 3)], yb.at[half, pl.ds(0, 3)],
         )
+        if half == 0:
+            turn_w.wait()
+            sums = [jnp.zeros((8, 128), F32) for _ in range(2)]
         for n in range(2):
             rows = pl.ds(pl.multiple_of(zh * 512 + n * 256, 256), 256)
             a = jnp.dot(h[0, rows, :], g[half], preferred_element_type=F32)
@@ -443,7 +468,19 @@
                 def _(to=to, st=st):
                     st.start(lax.rem(to - x + 4, 4))
 
+            for e in range(2):
+                to = 2 * n + e
+                vr, vi = yb[half, to, 0].astype(F32), yb[half, to, 1].astype(F32)
+                here = slice(half * 128, half * 128 + 128)
+                ar, ai = whrecv[to, 0, :, here].astype(F32), whrecv[to, 1, :, here].astype(F32)
+                sums[0] = sums[0] + fold(vr * ar - vi * ai)
+                sums[1] = sums[1] + fold(vr * ai + vi * ar)
+
         s[half, :, :, pl.ds(pl.multiple_of(x * 128, 128), 128)] = yb[half, x]
+        if half == 1:
+            for q in range(2):
+                irecv[1, 0, q] = jnp.sum(sums[q], axis=0, keepdims=True)
+            over = overlap(1)
         st.wait()
         lax.fori_loop(0, 4, functools.partial(columns, half), 0)
 
@@ -453,8 +490,7 @@
     def put_second(j, q, pair):
         prod[1, j, q] = pair
 
-    products(1, arr, put_second, lambda rows: (cs[0, rows, :], cs[1, rows, :]))
-    over = overlap(1)
+    products(1, arr, put_second, None)
     share = share_products(1)
     over.wait()
     weight = share_weights(1)
@@ -567,7 +603,9 @@
             pltpu.VMEM(block, BF16),
             pltpu.VMEM((2, *block), BF16),
             pltpu.VMEM((2, ROWS, GRID), F32),
-            pltpu.VMEM((2, ROWS, GRID), F32),
+            pltpu.VMEM(block, BF16),
+            pltpu.VMEM((4, 2, ROWS, 256), BF16),
+            pltpu.VMEM((4, 2, ROWS, 256), BF16),
             pltpu.VMEM((2, GRID, GRID), BF16),
             pltpu.VMEM((2, 2, GRID // 2, GRID), BF16),
             pltpu.VMEM(block, F32),

time: 128 us -> 128 us (level)
  no operation moved by 1% of the time
where the time goes in v6:
time: 128 us
  Pallas kernels  127 us (99%)
    pallas_call x1, Pallas kernels, on_device(): pl.pallas_call(kernel, out_shape=[jax.ShapeDtypeStruct(block, BF16)] * 3,...  126 us

profile of v6, /device:TPU:1, one launch (start us, length us, event | category | flops | bytes accessed | tf_op | source)
XLA Modules:
  0.0 127.8 jit_solution(16396436243832601853)
XLA Ops:
  0.6 126.0 %shard_map.85 = (bf16[2,128,1024]{2,1,0:T(8,128)(2,1)S(1)}, bf16[2,128,1024]{2,1,0:T(8,128)(2,1)S(1)}, bf16[2,128,1024]{2,1,0:T(8,128)(2,1)S(1)}) custom-call(bf16[2,128,1024]{2,1,0:T(8,128)(2,1)} %bitcast.4, bf16[2,128,1024]{2,1,0:T(8,128)(2,1)} %bitcast.5, bf16[2,128,1024]{2,1,0:T(8,128)(2,1)} %bitcast.6, f32[128,1024]{1,0:T(8,128)} %p1_in.1, ...), custom_call_target="tpu_custom_call" | custom-call | tf_op jit(solution)/shard_map/pallas_call | solution.py:597
  126.6 1.2 shard_map.86

commit v7 on v6

--- a/solution.py
+++ b/solution.py
@@ -321,11 +321,40 @@
     ]
     for c in own:
         c.start()
+    for c in loads[3:6]:
+        c.wait()
+
+    def turn_phase(j, _):
+        rows = sixteen(j)
+        c, sn = cos_sin(ph[1, rows, :])
+        br, bi = b[1, 0, rows, :].astype(F32), b[1, 1, rows, :].astype(F32)
+        w[0, rows, :] = (br * c + bi * sn).astype(BF16)
+        w[1, rows, :] = (br * sn - bi * c).astype(BF16)
+        return 0
+
+    lax.fori_loop(0, 8, turn_phase, 0)
+    turn_w = Stage(
+        lambda k: wh.at[lax.rem(x + k, 4)], lambda k: whrecv.at[x], x_peer,
+        whrecv.at[pl.ds(0, 3)], whrecv.at[pl.ds(0, 3)],
+    )
+
+    def adjoint(n, _):
+        cols = pl.ds(pl.multiple_of(n * 256, 256), 256)
+        field = w[...].reshape(2 * ROWS, GRID)
+        a = jnp.dot(field, h[0, :, cols], preferred_element_type=F32)
+        c = jnp.dot(field, h[1, :, cols], preferred_element_type=F32)
+        wh[n, 0] = (a[:ROWS] - c[ROWS:]).astype(BF16)
+        wh[n, 1] = (c[:ROWS] + a[ROWS:]).astype(BF16)
+        return 0
+
+    lax.fori_loop(0, 4, adjoint, 0)
     prod[0, pl.ds(2 * x, 2)] = px[x]
     turn.wait()
     share = share_products(0)
     for p in range(3):
         move(p, False)
+    turn_w.start_all(4)
+    whrecv[x] = wh[x]
     over.wait()
     weight = share_weights(0)
     raw[0, 0] = prod[0, yc]
@@ -382,35 +411,9 @@
     m1recv[x] = m1[pl.ds(2 * x, 2)]
     for c in own:
         c.wait()
-    for c in loads[3:]:
+    for c in loads[6:]:
         c.wait()
 
-    def turn_phase(j, _):
-        rows = sixteen(j)
-        c, sn = cos_sin(ph[1, rows, :])
-        br, bi = b[1, 0, rows, :].astype(F32), b[1, 1, rows, :].astype(F32)
-        w[0, rows, :] = (br * c + bi * sn).astype(BF16)
-        w[1, rows, :] = (br * sn - bi * c).astype(BF16)
-        return 0
-
-    lax.fori_loop(0, 8, turn_phase, 0)
-    turn_w = Stage(
-        lambda k: wh.at[lax.rem(x + k, 4)], lambda k: whrecv.at[x], x_peer,
-        whrecv.at[pl.ds(0, 3)], whrecv.at[pl.ds(0, 3)],
-    )
-
-    def adjoint(n, _):
-        cols = pl.ds(pl.multiple_of(n * 256, 256), 256)
-        field = w[...].reshape(2 * ROWS, GRID)
-        a = jnp.dot(field, h[0, :, cols], preferred_element_type=F32)
-        c = jnp.dot(field, h[1, :, cols], preferred_element_type=F32)
-        wh[n, 0] = (a[:ROWS] - c[ROWS:]).astype(BF16)
-        wh[n, 1] = (c[:ROWS] + a[ROWS:]).astype(BF16)
-        return 0
-
-    lax.fori_loop(0, 4, adjoint, 0)
-    turn_w.start_all(4)
-    whrecv[x] = wh[x]
 
     def columns(half, n, _):
         cols = pl.ds(pl.multiple_of(n * 256, 256), 256)

time: 128 us -> 122 us (0.953)
  Pallas kernels: 127 us -> 121 us
    pallas_call x1, Pallas kernels: 126 us -> 120 us  [on_device(): pl.pallas_call(kernel, out_shape=[jax.ShapeDtypeStruct(block, BF16)] * 3,...]
where the time goes in v7:
time: 122 us
  Pallas kernels  121 us (99%)
    pallas_call x1, Pallas kernels, on_device(): pl.pallas_call(kernel, out_shape=[jax.ShapeDtypeStruct(block, BF16)] * 3,...  120 us

profile of v7, /device:TPU:1, one launch (start us, length us, event | category | flops | bytes accessed | tf_op | source)
XLA Modules:
  0.0 122.1 jit_solution(16102018155915772939)
XLA Ops:
  0.6 120.2 %shard_map.85 = (bf16[2,128,1024]{2,1,0:T(8,128)(2,1)S(1)}, bf16[2,128,1024]{2,1,0:T(8,128)(2,1)S(1)}, bf16[2,128,1024]{2,1,0:T(8,128)(2,1)S(1)}) custom-call(bf16[2,128,1024]{2,1,0:T(8,128)(2,1)} %bitcast.4, bf16[2,128,1024]{2,1,0:T(8,128)(2,1)} %bitcast.5, bf16[2,128,1024]{2,1,0:T(8,128)(2,1)} %bitcast.6, f32[128,1024]{1,0:T(8,128)} %p1_in.1, ...), custom_call_target="tpu_custom_call" | custom-call | tf_op jit(solution)/shard_map/pallas_call | solution.py:600
  120.8 1.2 %shard_map.86 = (bf16[2,128,1024]{2,1,0:T(8,128)(2,1)}, bf16[2,128,1024]{2,1,0:T(8,128)(2,1)}, bf16[2,128,1024]{2,1,0:T(8,128)(2,1)}) custom-call(bf16[2,128,1024]{2,1,0:T(8,128)(2,1)S(1)} %get-tuple-element.9.refs_0_, bf16[2,128,1024]{2,1,0:T(8,128)(2,1)S(1)} %get-tuple-element.10.refs_1_, bf16[2,128,1024]{2,1,0:T(8,128)(2,1)S(1)} %get-tuple-element.11.refs_2_), custom_call_target="tpu_custom_call" | custom-call | tf_op jit(solution)/shard_map/pallas_call | solution.py:645

commit v8 on v7

--- a/solution.py
+++ b/solution.py
@@ -415,6 +415,8 @@
         c.wait()
 
 
+    to_rows = []
+
     def columns(half, n, _):
         cols = pl.ds(pl.multiple_of(n * 256, 256), 256)
         field = s[half].reshape(2 * ROWS, GRID // 2)
@@ -484,7 +486,10 @@
             for q in range(2):
                 irecv[1, 0, q] = jnp.sum(sums[q], axis=0, keepdims=True)
             over = overlap(1)
-        st.wait()
+        to_rows.append(st)
+
+    for half in range(2):
+        to_rows[half].wait()
         lax.fori_loop(0, 4, functools.partial(columns, half), 0)
 
     outs = [pltpu.make_async_copy(arr, a_out, ls.at[6])]

time: 122 us -> 122 us (level)
  no operation moved by 1% of the time
where the time goes in v8:
time: 122 us
  Pallas kernels  122 us (100%)
    pallas_call x1, Pallas kernels, on_device(): pl.pallas_call(kernel, out_shape=[jax.ShapeDtypeStruct(block, BF16)] * 3,...  120 us

profile of v8, /device:TPU:1, one launch (start us, length us, event | category | flops | bytes accessed | tf_op | source)
XLA Modules:
  0.0 122.3 jit_solution(17359940411740948757)
XLA Ops:
  0.6 120.4 %shard_map.85 = (bf16[2,128,1024]{2,1,0:T(8,128)(2,1)S(1)}, bf16[2,128,1024]{2,1,0:T(8,128)(2,1)S(1)}, bf16[2,128,1024]{2,1,0:T(8,128)(2,1)S(1)}) custom-call(bf16[2,128,1024]{2,1,0:T(8,128)(2,1)} %bitcast.4, bf16[2,128,1024]{2,1,0:T(8,128)(2,1)} %bitcast.5, bf16[2,128,1024]{2,1,0:T(8,128)(2,1)} %bitcast.6, f32[128,1024]{1,0:T(8,128)} %p1_in.1, ...), custom_call_target="tpu_custom_call" | custom-call | tf_op jit(solution)/shard_map/pallas_call | solution.py:605
  121.0 1.2 %shard_map.86 = (bf16[2,128,1024]{2,1,0:T(8,128)(2,1)}, bf16[2,128,1024]{2,1,0:T(8,128)(2,1)}, bf16[2,128,1024]{2,1,0:T(8,128)(2,1)}) custom-call(bf16[2,128,1024]{2,1,0:T(8,128)(2,1)S(1)} %get-tuple-element.9.refs_0_, bf16[2,128,1024]{2,1,0:T(8,128)(2,1)S(1)} %get-tuple-element.10.refs_1_, bf16[2,128,1024]{2,1,0:T(8,128)(2,1)S(1)} %get-tuple-element.11.refs_2_), custom_call_target="tpu_custom_call" | custom-call | tf_op jit(solution)/shard_map/pallas_call | solution.py:650
